TPU v7x, 32 devices: a whole 2x2x4 slice. The times are simulated.
32 devices in a mesh: grp: 4 (over y, x), seq: 8 (over z, core).
Axes of the slice: x: 2, y: 2, z: 4, core: 2. Of those that a mesh axis runs over, the one named last changes fastest.
Arguments:
- query_input: bfloat16 [4096, 4096], P(('grp', 'seq')), may hold values from -8 to 8
- key_input: bfloat16 [4096, 512], P(('grp', 'seq')), may hold values from -8 to 8
- value_input: bfloat16 [4096, 512], P(('grp', 'seq')), may hold values from -6 to 6
- out_grad: bfloat16 [4096, 4096], P(('grp', 'seq')), may hold values from -6 to 6
- key_blocks: int32 [32, 12], replicated, may hold values from 0 to 31, as said below
- key_counts: int32 [32], replicated, may hold values from 1 to 12, as said below
- block_position: int32 [32], replicated, may hold values from 0 to 31, each once
Outputs:
- attn_out: bfloat16 [4096, 4096], P(('grp', 'seq'))
- query_grad: bfloat16 [4096, 4096], P(('grp', 'seq'))
- key_grad: bfloat16 [4096, 512], P(('grp', 'seq'))
- value_grad: bfloat16 [4096, 512], P(('grp', 'seq'))
Inputs may be any that keep to these rules, and one draw needn't show every extreme that they name: `key_blocks`: in row b the first key_counts[b] entries are distinct, the first is b itself and the others are earlier blocks of the same group of 8 blocks or of the group before; the remaining entries equal b. `key_counts`: the last block's count is 12.
All inputs are finite; a program needn't handle non-finite values.
Results may differ from a plain program's by a relative error of at most 0.015.
Values may be sent and summed in bfloat16 or wider, within the bound.
No kernel may reach another device: no remote copies, remote signals or barrier semaphores. Data moves between devices by JAX's collectives and lax.ppermute only.
A program may use at most 128 MiB of HBM per device.

v0:
```python
import functools
import math

import jax
import jax.numpy as jnp
import numpy as np
from jax import lax
from jax.experimental import pallas as pl
from jax.experimental.pallas import tpu as pltpu
from jax.sharding import PartitionSpec as P

HEADS = 32
KV_HEADS = 4
HEAD_DIM = 128
BLK = 128
CORES = 2
RATIO = HEADS // KV_HEADS
HALF_KV = KV_HEADS // CORES
ROWS = RATIO * BLK
SCALE = 1.0 / math.sqrt(HEAD_DIM)
TO_LOG2 = SCALE * math.log2(math.e)
F32 = jnp.float32
BF16 = jnp.bfloat16
CHUNK = 256

VMEM_SPEC = pl.BlockSpec(memory_space=pltpu.VMEM)
HBM_SPEC = pl.BlockSpec(memory_space=pltpu.HBM)
SMEM_SPEC = pl.BlockSpec(memory_space=pltpu.SMEM)


def trig_table(n_blocks):
    half = HEAD_DIM // 2
    frequency = np.power(500000.0, -np.arange(half) * (2.0 / HEAD_DIM))
    parts = []
    for places in (np.arange(n_blocks) * BLK, np.arange(BLK)):
        angles = places[:, None] * frequency
        for part in (np.cos(angles), np.sin(angles)):
            parts.append(np.concatenate([part, part], axis=1))
    return np.concatenate(parts, axis=0).astype(np.float32)


def block_tables(place, table):
    n_blocks = table.shape[0] // 2 - BLK
    cos_b = table[pl.ds(place, 1), :]
    sin_b = table[pl.ds(n_blocks + place, 1), :]
    cos_t = table[2 * n_blocks : 2 * n_blocks + BLK, :]
    sin_t = table[2 * n_blocks + BLK :, :]
    cosine = cos_b * cos_t - sin_b * sin_t
    sine = sin_b * cos_t + cos_b * sin_t
    lanes = lax.broadcasted_iota(jnp.int32, sine.shape, 1)
    return cosine, jnp.where(lanes < HEAD_DIM // 2, -sine, sine)


def turn(values, cosine, signed_sine):
    return values * cosine + pltpu.roll(values, HEAD_DIM // 2, 1) * signed_sine


def dot_nt(a, b):
    return lax.dot_general(a, b, (((1,), (1,)), ((), ())), preferred_element_type=F32)


def dot_nn(a, b):
    return lax.dot_general(a, b, (((1,), (0,)), ((), ())), preferred_element_type=F32)


def here(n_seq):
    member = lax.axis_index("seq")
    group = lax.axis_index("grp")
    return group, member, lax.rem(member, CORES)


def size_of(array):
    return math.prod(array.shape) * jnp.dtype(array.dtype).itemsize


def call(kernel, out_shape, n_smem, scratch=(), us=1, name=None, n_hbm=0, hbm_out=None, pin=False):
    def placed(n, a):
        if n == hbm_out:
            return pltpu.HBM(a.shape, a.dtype)
        return pltpu.VMEM(a.shape, a.dtype) if pin else a

    def spec(n, a):
        if a.dtype == jnp.int32:
            return SMEM_SPEC
        return HBM_SPEC if n == hbm_out else VMEM_SPEC

    def run(*arrays):
        n_left = n_smem + n_hbm
        outs = list(out_shape) if isinstance(out_shape, (tuple, list)) else [out_shape]
        held = sum(size_of(a) for a in arrays[n_left:])
        held += sum(size_of(a) for n, a in enumerate(outs) if n != hbm_out)
        held += sum(size_of(a) for a in scratch if a.dtype in (F32, BF16))
        in_specs = [SMEM_SPEC] * n_smem + [HBM_SPEC] * n_hbm
        in_specs += [VMEM_SPEC] * (len(arrays) - n_left)
        pinned = [
            pltpu.with_memory_space_constraint(a, pltpu.HBM) if n < n_left else a
            for n, a in enumerate(arrays)
        ]
        results = pl.pallas_call(
            kernel,
            out_shape=[placed(n, a) for n, a in enumerate(outs)],
            in_specs=in_specs,
            out_specs=[spec(n, a) for n, a in enumerate(outs)],
            scratch_shapes=list(scratch),
            compiler_params=pltpu.CompilerParams(vmem_limit_bytes=held + 6 * 2**20),
            cost_estimate=pl.CostEstimate(
                flops=us * 10**9, bytes_accessed=2**20, transcendentals=0
            ),
            name=name,
        )(*pinned)
        return results if isinstance(out_shape, (tuple, list)) else results[0]

    return run


def fetch(sources, places, sems):
    copies = [
        pltpu.make_async_copy(source, place, sems.at[n])
        for n, (source, place) in enumerate(zip(sources, places))
    ]
    for copy in copies:
        copy.start()
    for copy in copies:
        copy.wait()


def prepare_kv(n_seq, place_ref, *refs):
    sources, (keep, send), (key, value, table, sems) = refs[:3], refs[3:5], refs[5:]
    fetch(sources, (key, value, table), sems)
    group, member, core = here(n_seq)
    cosine, sine = block_tables(place_ref[group * n_seq + member], table)
    for out, half in ((keep, core), (send, 1 - core)):
        for h in range(HALF_KV):
            columns = pl.ds(pl.multiple_of((half * HALF_KV + h) * HEAD_DIM, HEAD_DIM), HEAD_DIM)
            out[0, h] = turn(key[:, columns].astype(F32), cosine, sine).astype(BF16)
            out[1, h] = value[:, columns]


def prepare_queries(n_seq, place_ref, *refs):
    sources, (keep, send), (query, grad, table, sems) = refs[:3], refs[3:5], refs[5:]
    fetch(sources, (query, grad, table), sems)
    group, member, core = here(n_seq)
    cosine, sine = block_tables(place_ref[group * n_seq + member], table)
    for out, half in ((keep, core), (send, 1 - core)):
        for h in range(HALF_KV):
            for r in range(RATIO):
                head = (half * HALF_KV + h) * RATIO + r
                columns = pl.ds(pl.multiple_of(head * HEAD_DIM, HEAD_DIM), HEAD_DIM)
                out[0, h, r] = turn(query[:, columns].astype(F32), cosine, sine).astype(BF16)
                out[1, h, r] = grad[:, columns]


def make_lists(n_seq, split, key_blocks, key_counts, lists, counts):
    group, member, _ = here(n_seq)
    for i in range(2):
        block = group * n_seq + lax.bitwise_xor(member, i)
        for section in range(3):
            counts[i, section] = int(section == 1)
        lists[i, 1, 0] = i

        def look(j, _):
            place = lax.bitwise_xor(key_blocks[block, j] - (group - 1) * n_seq, member)
            section = (place >= n_seq).astype(jnp.int32)
            section += (place >= n_seq + split).astype(jnp.int32)
            n = counts[i, section]
            lists[i, section, n] = place - jnp.where(section == 0, 0, n_seq) - jnp.where(
                section == 2, split, 0
            )
            counts[i, section] = n + 1
            return 0

        lax.fori_loop(1, key_counts[block], look, 0)
        total = 0
        for section, base in enumerate((0, n_seq, n_seq + split)):

            def append(n, m):
                lists[i, 3, m] = lists[i, section, n] + base
                return m + 1

            total = lax.fori_loop(0, counts[i, section], append, jnp.int32(total))
        counts[i, 3] = total
        lists[i, 3, total] = 0


def causal():
    keys = lax.broadcasted_iota(jnp.int32, (BLK, CHUNK), 0)
    tokens = lax.rem(lax.broadcasted_iota(jnp.int32, (BLK, CHUNK), 1), BLK)
    return keys <= tokens


def chunks():
    per = CHUNK // BLK
    return [
        (slice(c * per, (c + 1) * per), slice(c * CHUNK, (c + 1) * CHUNK))
        for c in range(ROWS // CHUNK)
    ]


def heads_of(block, what, h, rows):
    return block[what, h, rows].reshape(CHUNK, HEAD_DIM)


def fill(store, pieces, first=0):
    for k, piece in enumerate(pieces):
        store[first + CORES * k : first + CORES * (k + 1)] = piece[...]


def pair_scores(store, e, h, block, rows, diagonal):
    scores = dot_nt(store[e, 0, h], heads_of(block, 0, h, rows))
    if diagonal:
        scores = jnp.where(causal(), scores, -1e30)
    return scores, dot_nt(store[e, 1, h], heads_of(block, 1, h, rows))


def gather_stats(store, e, block, stats, i, diagonal, kept=None):
    for h in range(HALF_KV):
        for rows, columns in chunks():
            scores, dprobs = pair_scores(store, e, h, block, rows, diagonal)
            if kept is not None:
                n, kept_scores, kept_dprobs = kept
                kept_scores[n, h, :, columns] = scores
                kept_dprobs[n, h, :, columns] = dprobs
            top = jnp.max(scores, axis=0, keepdims=True)
            if not diagonal:
                old_top = stats[i, h, 0:1, columns]
                top = jnp.maximum(top, old_top)
            weights = jnp.exp2((scores - top) * TO_LOG2)
            total = jnp.sum(weights, axis=0, keepdims=True)
            mixed = jnp.sum(weights * dprobs, axis=0, keepdims=True)
            if not diagonal:
                shrink = jnp.exp2((old_top - top) * TO_LOG2)
                total += stats[i, h, 1:2, columns] * shrink
                mixed += stats[i, h, 2:3, columns] * shrink
            stats[i, h, 0:1, columns] = top
            stats[i, h, 1:2, columns] = total
            stats[i, h, 2:3, columns] = mixed


def spread_grads(found, count, kept_scores, kept_dprobs, stats, i, block, acc, saved, low, sent):
    def copy(n):
        return pltpu.make_async_copy(low.at[n], saved.at[i, n], sent.at[n])

    def add(n, _):
        e = found[n]
        for h in range(HALF_KV):
            dk, dv = acc[e, 0, h], acc[e, 1, h]
            for rows, columns in chunks():
                probs = jnp.exp2(
                    kept_scores[n, h, :, columns] * TO_LOG2 - stats[i, h, 0:1, columns]
                )
                dscores = probs * (kept_dprobs[n, h, :, columns] - stats[i, h, 2:3, columns])
                probs, dscores = probs.astype(BF16), dscores.astype(BF16)
                low[n, h, 0, :, columns] = probs
                low[n, h, 1, :, columns] = dscores
                dv += dot_nn(probs, heads_of(block, 1, h, rows))
                dk += dot_nn(dscores, heads_of(block, 0, h, rows))
            acc[e, 0, h] = dk
            acc[e, 1, h] = dv
        copy(n).start()
        return 0

    def finish(n, _):
        copy(n).wait()
        return 0

    lax.fori_loop(0, count, add, 0)
    lax.fori_loop(0, count, finish, 0)


def write_grads(acc, outs):
    start = 0
    for out in outs:
        part = slice(start, start + out.shape[0])
        out[:, 0] = (acc[part, 0] * SCALE).astype(out.dtype)
        out[:, 1] = acc[part, 1].astype(out.dtype)
        start += out.shape[0]


def current_stats(section, lists, counts, own, other, *rest):
    *pieces, stats, store = rest
    first = section == 1
    if not first:
        stats_in, *pieces = pieces
        stats[...] = stats_in[...]
    fill(store, pieces)
    for i, block in enumerate((own, other)):
        if first:
            gather_stats(store, i, block, stats, i, True)

        def step(n, _):
            gather_stats(store, lists[i, section, n], block, stats, i, False)
            return 0

        lax.fori_loop(int(first), counts[i, section], step, 0)


def previous_grads(n_pieces, lists, counts, own, other, stats_in, *rest):
    n_ends = 2 * n_pieces - 1
    pieces, outs = rest[:n_pieces], rest[n_pieces:n_ends]
    saved, stats, store, acc, low, sent, kept_scores, kept_dprobs = rest[n_ends:]
    fill(store, pieces)
    acc[...] = jnp.zeros_like(acc)
    stats[...] = stats_in[...]
    for i, block in enumerate((own, other)):
        count = counts[i, 0]

        def look(n, _):
            gather_stats(
                store, lists[i, 0, n], block, stats, i, False, (n, kept_scores, kept_dprobs)
            )
            return 0

        lax.fori_loop(0, count, look, 0)
        for h in range(HALF_KV):
            total = stats[i, h, 1:2, :]
            stats[i, h, 0:1, :] = stats[i, h, 0:1, :] * TO_LOG2 + jnp.log2(total)
            stats[i, h, 2:3, :] = stats[i, h, 2:3, :] / total

        def copy(n):
            return pltpu.make_async_copy(low.at[n], saved.at[i, n], sent.at[n])

        def add(n, _):
            e = lists[i, 0, n]
            for h in range(HALF_KV):
                dk, dv = acc[e, 0, h], acc[e, 1, h]
                for rows, columns in chunks():
                    probs = jnp.exp2(
                        kept_scores[n, h, :, columns] * TO_LOG2 - stats[i, h, 0:1, columns]
                    )
                    dscores = probs * (kept_dprobs[n, h, :, columns] - stats[i, h, 2:3, columns])
                    probs, dscores = probs.astype(BF16), dscores.astype(BF16)
                    low[n, h, 0, :, columns] = probs
                    low[n, h, 1, :, columns] = dscores
                    dv += dot_nn(probs, heads_of(block, 1, h, rows))
                    dk += dot_nn(dscores, heads_of(block, 0, h, rows))
                acc[e, 0, h] = dk
                acc[e, 1, h] = dv
            copy(n).start()
            return 0

        def finish(n, _):
            copy(n).wait()
            return 0

        lax.fori_loop(0, count, add, 0)
        lax.fori_loop(0, count, finish, 0)
    write_grads(acc, outs)


def current_grads(section, n_pieces, lists, counts, own, other, stats, *rest):
    pieces, outs = rest[:n_pieces], rest[n_pieces : 2 * n_pieces]
    saved, store, acc, low, sent = rest[2 * n_pieces :]
    first = section == 1
    fill(store, pieces)
    acc[...] = jnp.zeros_like(acc)
    for i, block in enumerate((own, other)):
        count = counts[i, section]

        def copy(n):
            return pltpu.make_async_copy(low.at[n], saved.at[i, n], sent.at[n])

        def look(n, diagonal):
            e = lists[i, section, n]
            for h in range(HALF_KV):
                for rows, columns in chunks():
                    scores, dprobs = pair_scores(store, e, h, block, rows, diagonal)
                    probs = jnp.exp2(scores * TO_LOG2 - stats[i, h, 0:1, columns])
                    low[n, h, 0, :, columns] = probs.astype(BF16)
                    dscores = probs * (dprobs - stats[i, h, 2:3, columns])
                    low[n, h, 1, :, columns] = dscores.astype(BF16)
            copy(n).start()
            return 0

        def add(n, _):
            e = lists[i, section, n]
            for h in range(HALF_KV):
                for w in range(2):
                    right = block[1 - w, h].reshape(ROWS, HEAD_DIM)
                    acc[e, 1 - w, h] += dot_nn(low[n, h, w], right)
            return 0

        def finish(n, _):
            copy(n).wait()
            return 0

        if first:
            look(0, True)
        lax.fori_loop(int(first), count, lambda n, _: look(n, False), 0)
        lax.fori_loop(0, count, add, 0)
        lax.fori_loop(0, count, finish, 0)
    write_grads(acc, outs)


def query_results(n_seq, lists, counts, place_ref, *rest):
    n_saved = 3
    n_pieces = n_seq // CORES
    saved, pieces, rest = rest[:n_saved], rest[n_saved:][: 2 * n_pieces], rest[n_saved + 2 * n_pieces :]
    table, *rest = rest
    outs, (store, low, out_acc, dq_acc, got) = rest[: 2 * HALF_KV], rest[2 * HALF_KV :]
    group, member, _ = here(n_seq)

    def copy(source, h, i, n, first):
        return pltpu.make_async_copy(source.at[i, n - first, h], low.at[h, i, n], got.at[h, i, n])

    ends = []
    for i in range(2):
        stops = [0]
        for section in range(n_saved):
            stops.append(stops[-1] + counts[i, section])
        ends.append(stops)
    for h in range(HALF_KV):
        for i, stops in enumerate(ends):
            for source, first, stop in zip(saved, stops, stops[1:]):

                def fetch_one(n, _):
                    copy(source, h, i, n, first).start()
                    return 0

                lax.fori_loop(first, stop, fetch_one, 0)
    fill(store, pieces)
    tables = []
    for i in range(2):
        mine = group * n_seq + lax.bitwise_xor(member, i)
        cosine, sine = block_tables(place_ref[mine], table)
        tables.append((cosine.T * SCALE, sine.T * SCALE))
    for h, (i, stops) in ((h, pair) for h in range(HALF_KV) for pair in enumerate(ends)):
        total = stops[-1]
        result = outs[i * HALF_KV + h]

        @pl.when(lax.rem(total, 2) == 1)
        def _():
            low[h, i, total] = jnp.zeros((2, BLK, ROWS), BF16)

        out_acc[...] = jnp.zeros_like(out_acc)
        dq_acc[...] = jnp.zeros_like(dq_acc)

        def add(n, _):
            pair = (2 * n, 2 * n + 1)
            for m in pair:
                for source, first, stop in zip(saved, stops, stops[1:]):

                    @pl.when(jnp.logical_and(m >= first, m < stop))
                    def _():
                        copy(source, h, i, m, first).wait()

            found = [lists[i, 3, m] for m in pair]
            keys_t = jnp.concatenate([store[e, 0, h].T for e in found], axis=1)
            values_t = jnp.concatenate([store[e, 1, h].T for e in found], axis=1)
            for _, columns in chunks():
                probs = jnp.concatenate([low[h, i, m, 0, :, columns] for m in pair], axis=0)
                dscores = jnp.concatenate([low[h, i, m, 1, :, columns] for m in pair], axis=0)
                out_acc[:, columns] += dot_nn(values_t, probs)
                dq_acc[:, columns] += dot_nn(keys_t, dscores)
            return 0

        lax.fori_loop(0, lax.div(total + 1, 2), add, 0)
        cosine, sine = tables[i]
        for r in range(RATIO):
            rows = slice(r * BLK, (r + 1) * BLK)
            columns = slice(r * HEAD_DIM, (r + 1) * HEAD_DIM)
            result[0, :, columns] = out_acc[:, rows].astype(BF16).T
            dq = dq_acc[:, rows]
            half = HEAD_DIM // 2
            turned = jnp.concatenate([dq[half:], dq[:half]], axis=0)
            result[1, :, columns] = (dq * cosine - turned * sine).astype(BF16).T


def finish_kv(n_seq, place_ref, *rest):
    *terms, table, keep, send = rest
    group, member, _ = here(n_seq)
    for i, result in enumerate((keep, send)):
        offset = lax.bitwise_xor(member, i)
        cosine, sine = block_tables(place_ref[group * n_seq + offset], table)
        for h in range(HALF_KV):
            columns = slice(h * HEAD_DIM, (h + 1) * HEAD_DIM)
            dk, dv = (sum(term[i, w, h].astype(F32) for term in terms) for w in range(2))
            result[0, :, columns] = turn(dk, cosine, -sine).astype(BF16)
            result[1, :, columns] = dv.astype(BF16)


def join_halves(*refs):
    core = lax.rem(lax.axis_index("seq"), CORES)
    own_q, got_q, (own_kv, got_kv) = refs[:HALF_KV], refs[HALF_KV:][:HALF_KV], refs[2 * HALF_KV :][:2]
    outs = refs[2 * HALF_KV + 2 :]
    for own, got, results in ((own_q, got_q, outs[:2]), ([own_kv], [got_kv], outs[2:])):
        width = own[0].shape[-1]
        for half, parts in ((core, own), (1 - core, got)):
            for n, part in enumerate(parts):
                start = pl.multiple_of((half * len(parts) + n) * width, width)
                for w, out in enumerate(results):
                    out[:, pl.ds(start, width)] = part[w]


def local(query_input, key_input, value_input, out_grad, key_blocks, key_counts, block_position):
    n_seq = lax.axis_size("seq")
    n_grp = lax.axis_size("grp")
    n_pieces = n_seq // CORES
    n_listed = key_blocks.shape[1]

    def cross(array, by):
        return lax.ppermute(array, "seq", [(m, m ^ by) for m in range(n_seq)])

    def along(array, by):
        return cross(array, CORES * by)

    def onward(array):
        return lax.ppermute(array, "grp", [(g, g + 1) for g in range(n_grp - 1)])

    def back(array):
        return lax.ppermute(array, "grp", [(g + 1, g) for g in range(n_grp - 1)])

    table = trig_table(block_position.shape[0])
    n_far = min(n_seq, n_listed - 1)
    split = 2 * CORES
    piece = (2, HALF_KV, BLK, HEAD_DIM)
    chip = (CORES, *piece)
    q_shape = jax.ShapeDtypeStruct((2, HALF_KV, RATIO, BLK, HEAD_DIM), BF16)
    kv_shape = jax.ShapeDtypeStruct(piece, BF16)
    stats_shape = jax.ShapeDtypeStruct((2, HALF_KV, 8, ROWS), F32)
    low = jax.ShapeDtypeStruct(chip, BF16)
    high = jax.ShapeDtypeStruct(chip, F32)
    lists, counts = call(
        functools.partial(make_lists, n_seq, split),
        (
            jax.ShapeDtypeStruct((2, 4, n_listed + 1), jnp.int32),
            jax.ShapeDtypeStruct((2, 4), jnp.int32),
        ),
        2, us=2, name="block_lists",
    )(key_blocks, key_counts)

    def prepared(kernel, shape, first, second, name):
        held = [pltpu.VMEM(a.shape, a.dtype) for a in (first, second, table)]
        return call(
            functools.partial(kernel, n_seq), (shape, shape), 1,
            [*held, pltpu.SemaphoreType.DMA((3,))], us=1, name=name, n_hbm=3, pin=True,
        )(block_position, first, second, table)

    kv_keep, kv_send = prepared(prepare_kv, kv_shape, key_input, value_input, "rotate_keys")
    kv_got = cross(kv_send, 1)
    query_late, kv_keep = lax.optimization_barrier((query_input, kv_keep))
    q_keep, q_send = prepared(prepare_queries, q_shape, query_late, out_grad, "rotate_queries")
    q_send, q_keep, kv_got, kv_keep = lax.optimization_barrier((q_send, q_keep, kv_got, kv_keep))
    q_got = cross(q_send, 1)
    near = [jnp.stack([kv_keep, kv_got])]
    near.append(along(near[0], 1))
    ready, first_far = lax.optimization_barrier((near[1], onward(near[0])))
    far = [first_far, None]
    for k in range(2, n_pieces, 2):
        piece_k, _ = lax.optimization_barrier((along(near[0], k), ready))
        near += [piece_k, along(piece_k, 1)]
        far += [onward(piece_k), None]
    stats = call(
        functools.partial(current_stats, 1), stats_shape, 2, [pltpu.VMEM((split, *piece), BF16)],
        us=4, name="near_statistics",
    )(lists, counts, q_keep, q_got, *near[:2])
    ready, far[2], stats = lax.optimization_barrier((ready, far[2], stats))
    far[1] = onward(ready)
    for k in range(2, n_pieces, 2):
        far[k + 1] = along(far[k], 1)
    stats = call(
        functools.partial(current_stats, 2), stats_shape, 2,
        [pltpu.VMEM((n_seq - split, *piece), BF16)], us=4, name="far_statistics",
    )(lists, counts, q_keep, q_got, stats, *near[2:])

    def grads_call(kernel, n_slots, n_store, outs, us, name, kept=(), more=()):
        pair = (n_slots, HALF_KV, 2, BLK, ROWS)
        saved = jax.ShapeDtypeStruct((2, *pair), BF16)
        return call(
            kernel, (*outs, saved, *more), 2,
            [
                pltpu.VMEM((n_store, *piece), BF16), pltpu.VMEM((n_store, *piece), F32),
                pltpu.VMEM(pair, BF16), pltpu.SemaphoreType.DMA((n_slots,)), *kept,
            ],
            us=us, name=name, hbm_out=len(outs),
        )

    kept = pltpu.VMEM((n_far, HALF_KV, BLK, ROWS), F32)
    two = jax.ShapeDtypeStruct((2 * CORES, *piece), BF16)
    first_far, *far_grads, far_saved, stats = grads_call(
        functools.partial(previous_grads, n_pieces), n_far, n_seq, (two,) + (low,) * (n_pieces - 2),
        14, "previous_gradients", (kept, kept), (stats_shape,),
    )(lists, counts, q_keep, q_got, stats, *far)

    def current_call(section, outs, name, pieces, after):
        stats_late, _ = lax.optimization_barrier((stats, after))
        n_store = CORES * len(pieces)
        *grads, saved = grads_call(
            functools.partial(current_grads, section, len(pieces)), min(n_store, n_listed), n_store,
            outs, 6, name,
        )(lists, counts, q_keep, q_got, stats_late, *pieces)
        return grads, saved

    def total(*terms):
        return sum(term.astype(F32) for term in terms).astype(BF16)

    from_far = back(first_far)
    crossing = [along(grad, 1) for grad in far_grads[1::2]]
    high_grads, high_saved = current_call(
        2, [high, low] * (n_pieces // 2 - 1), "far_current_gradients", near[2:], far_grads[0]
    )
    crossing, high_grads = lax.optimization_barrier((crossing, high_grads))
    arrived = [
        back(total(grad, extra)) for grad, extra in zip(far_grads[0::2], crossing)
    ]
    swapped = [along(grad, 1) for grad in high_grads[1::2]]
    low_grads, low_saved = current_call(
        1, [high, high], "near_current_gradients", near[:2], high_grads[0]
    )
    low_grads, from_far = lax.optimization_barrier((low_grads, from_far))
    from_next = along(total(low_grads[1], from_far[CORES:]), 1)
    merged = [
        total(*terms) for terms in zip(high_grads[0::2], arrived, swapped)
    ]
    half_out = jax.ShapeDtypeStruct((2, BLK, RATIO * HEAD_DIM), BF16)
    place_late, _ = lax.optimization_barrier((block_position, merged))
    wide = pltpu.VMEM((HEAD_DIM, ROWS), F32)
    slots = (HALF_KV, 2, n_listed + 1)
    halves = call(
        functools.partial(query_results, n_seq), (half_out,) * (2 * HALF_KV), 3,
        [
            pltpu.VMEM((2 * n_seq, *piece), BF16), pltpu.VMEM((*slots, 2, BLK, ROWS), BF16),
            wide, wide, pltpu.SemaphoreType.DMA(slots),
        ],
        us=20, name="query_results", n_hbm=3,
    )(lists, counts, place_late, far_saved, low_saved, high_saved, *far, *near, table)
    own_halves, other_halves = halves[:HALF_KV], halves[HALF_KV:]
    other_halves = lax.optimization_barrier(list(other_halves))
    got_halves = [cross(half, 1) for half in other_halves]
    final = [low_grads[0], from_far[:CORES], from_next]
    final += [along(part, 2 + 2 * n) for n, part in enumerate(merged)]
    own_halves = list(own_halves)
    final[0], own_halves[1] = lax.optimization_barrier((final[0], own_halves[1]))
    kv_half = jax.ShapeDtypeStruct((2, BLK, HALF_KV * HEAD_DIM), BF16)
    own_kv, other_kv = call(
        functools.partial(finish_kv, n_seq), (kv_half, kv_half), 1, us=2, name="key_gradients"
    )(block_position, *final, table)
    got_kv = cross(other_kv, 1)
    q_out = jax.ShapeDtypeStruct(query_input.shape, BF16)
    kv_out = jax.ShapeDtypeStruct(key_input.shape, BF16)
    out_rows, query_grad, key_grad, value_grad = call(
        join_halves, (q_out, q_out, kv_out, kv_out), 0, us=2, name="join_halves"
    )(*own_halves, *got_halves, own_kv, got_kv)
    return (out_rows, query_grad, key_grad, value_grad)


def solution(mesh):
    split = P(("grp", "seq"), None)
    return jax.shard_map(
        local,
        mesh=mesh,
        in_specs=(split, split, split, split, P(), P(), P()),
        out_specs=(split, split, split, split),
        check_vma=False,
    )
```

profile of v0, /device:TPU:5, one launch (start us, length us, event | category | flops | bytes accessed | tf_op | source)
XLA Modules:
  0.0 101.1 jit_solution(9921944686385937385)
XLA Ops:
  0.6 1.9 %rotate_keys.1 = (bf16[2,2,128,128]{3,2,1,0:T(8,128)(2,1)S(1)}, bf16[2,2,128,128]{3,2,1,0:T(8,128)(2,1)S(1)}) custom-call(s32[32]{0:T(128)} %place_ref.6, bf16[128,512]{1,0:T(8,128)(2,1)} %refs_0_.1, bf16[128,512]{1,0:T(8,128)(2,1)} %refs_1_.2, f32[320,128]{1,0:T(8,128)} %constant.2.clone.refs_2_.rest_11_.rest_4_), custom_call_target="tpu_custom_call" | custom-call | flops 1000000000 | bytes 1048576 | tf_op jit(solution)/shard_map/rotate_keys/pallas_call | solution.py:99
  2.5 0.7 collective-permute-start
  3.2 3.0 %rotate_queries.1 = (bf16[2,2,8,128,128]{4,3,2,1,0:T(8,128)(2,1)S(1)}, bf16[2,2,8,128,128]{4,3,2,1,0:T(8,128)(2,1)S(1)}) custom-call(s32[32]{0:T(128)} %place_ref.6, bf16[128,4096]{1,0:T(8,128)(2,1)} %refs_0_.2, bf16[128,4096]{1,0:T(8,128)(2,1)} %refs_1_.3, f32[320,128]{1,0:T(8,128)} %constant.2.clone.refs_2_.rest_11_.rest_4_), custom_call_target="tpu_custom_call" | custom-call | flops 1000000000 | bytes 1048576 | tf_op jit(solution)/shard_map/rotate_queries/pallas_call | solution.py:99
  6.3 0.0 copy-start.1
  6.3 1.0 copy-done.1
  7.2 0.0 collective-permute-done
  7.2 0.0 collective-permute-start.1
  7.3 3.1 %collective-permute-start.3 = (bf16[2,2,2,128,128]{4,3,2,1,0:T(8,128)(2,1)S(1)}, bf16[2,2,2,128,128]{4,3,2,1,0:T(8,128)(2,1)S(1)}, u32[]{:S(2)}, u32[]{:S(2)}) collective-permute-start(bf16[2,2,2,128,128]{4,3,2,1,0:T(8,128)(2,1)S(1)} %pad_maximum_fusion.rest_0_.rest_7_), channel_id=1, source_target_pairs={{0,8},{8,16},{16,24},{1,9},{9,17},{17,25},{2,10},{10,18},{18,26},{... | collective-permute-start | bytes 786440 | tf_op jit(solution)/shard_map/ppermute | solution.py:507
  10.4 1.4 %collective-permute-start.2 = (bf16[2,2,2,128,128]{4,3,2,1,0:T(8,128)(2,1)S(1)}, bf16[2,2,2,128,128]{4,3,2,1,0:T(8,128)(2,1)S(1)}, u32[]{:S(2)}, u32[]{:S(2)}) collective-permute-start(bf16[2,2,2,128,128]{4,3,2,1,0:T(8,128)(2,1)S(1)} %pad_maximum_fusion.rest_0_.rest_7_), channel_id=1, source_target_pairs={{0,2},{1,3},{2,0},{3,1},{4,6},{5,7},{6,4},{7,5},{8,10},{9,11},{10,... | collective-permute-start | bytes 786440 | tf_op jit(solution)/shard_map/ppermute | solution.py:501
  11.8 2.3 %collective-permute-start.4 = (bf16[2,2,2,128,128]{4,3,2,1,0:T(8,128)(2,1)S(1)}, bf16[2,2,2,128,128]{4,3,2,1,0:T(8,128)(2,1)S(1)}, u32[]{:S(2)}, u32[]{:S(2)}) collective-permute-start(bf16[2,2,2,128,128]{4,3,2,1,0:T(8,128)(2,1)S(1)} %pad_maximum_fusion.rest_0_.rest_7_), channel_id=1, source_target_pairs={{0,4},{1,5},{2,6},{3,7},{4,0},{5,1},{6,2},{7,3},{8,12},{9,13},{10,... | collective-permute-start | bytes 786440 | tf_op jit(solution)/shard_map/ppermute | solution.py:501
  14.1 1.4 %copy.12.key_blocks = s32[32,12]{1,0:T(8,128)} copy(s32[32,12]{0,1:T(8,128)} %param.12) | data formatting | bytes 3072 | tf_op args[4]
  15.5 2.0 %block_lists.1 = (s32[2,4,13]{2,1,0:T(4,128)S(1)}, s32[2,4]{1,0:T(2,128)S(1)}) custom-call(s32[32,12]{1,0:T(8,128)} %copy.12.key_blocks, s32[32]{0:T(128)} %key_counts.1), custom_call_target="tpu_custom_call" | custom-call | flops 2000000000 | bytes 1048576 | tf_op jit(solution)/shard_map/block_lists/pallas_call | solution.py:99
  17.5 0.0 copy-start.3
  17.5 0.6 copy-done.3
  18.1 0.0 copy-start.4
  18.1 0.0 collective-permute-done.3.rest_0_.rest_3_
  18.1 5.0 %collective-permute-done.2.rest_1_.rest_8_ = bf16[2,2,2,128,128]{4,3,2,1,0:T(8,128)(2,1)S(1)} collective-permute-done((bf16[2,2,2,128,128]{4,3,2,1,0:T(8,128)(2,1)S(1)}, bf16[2,2,2,128,128]{4,3,2,1,0:T(8,128)(2,1)S(1)}, u32[]{:S(2)}, u32[]{:S(2)}) %collective-permute-start.2) | collective-permute-done | bytes 262176 | tf_op jit(solution)/shard_map/ppermute | solution.py:501
  23.0 0.0 collective-permute-done.4.rest_1_.rest_0_.rest_9_
  23.0 2.5 %collective-permute-start.6 = (bf16[2,2,2,128,128]{4,3,2,1,0:T(8,128)(2,1)S(1)}, bf16[2,2,2,128,128]{4,3,2,1,0:T(8,128)(2,1)S(1)}, u32[]{:S(2)}, u32[]{:S(2)}) collective-permute-start(bf16[2,2,2,128,128]{4,3,2,1,0:T(8,128)(2,1)S(1)} %collective-permute-done.4.rest_1_.rest_0_.rest_9_), channel_id=1, source_target_pairs={{0,2},{1,3},{2,0},{3,1},{4,6},{5,7},{6,4},{7,5},{8,10},{9,11},{10,... | collective-permute-start | bytes 786440 | tf_op jit(solution)/shard_map/ppermute | solution.py:501
  25.5 1.9 %collective-permute-start.5 = (bf16[2,2,2,128,128]{4,3,2,1,0:T(8,128)(2,1)S(1)}, bf16[2,2,2,128,128]{4,3,2,1,0:T(8,128)(2,1)S(1)}, u32[]{:S(2)}, u32[]{:S(2)}) collective-permute-start(bf16[2,2,2,128,128]{4,3,2,1,0:T(8,128)(2,1)S(1)} %collective-permute-done.4.rest_1_.rest_0_.rest_9_), channel_id=1, source_target_pairs={{0,8},{8,16},{16,24},{1,9},{9,17},{17,25},{2,10},{10,18},{18,26},{... | collective-permute-start | bytes 786440 | tf_op jit(solution)/shard_map/ppermute | solution.py:507
  27.4 0.0 collective-permute-done.1.other
  27.4 0.0 copy-done.4
  27.4 0.0 copy-start.2
  27.5 1.2 %copy-done.2 = bf16[2,2,8,128,128]{4,3,2,1,0:T(8,128)(2,1)S(1)} copy-done((bf16[2,2,8,128,128]{4,3,2,1,0:T(8,128)(2,1)S(1)}, bf16[2,2,8,128,128]{4,3,2,1,0:T(8,128)(2,1)}, u32[]{:S(2)}) %copy-start.2) | copy-done | bytes 1048600
  28.7 1.9 %near_statistics.1.rest_0_ = f32[2,2,8,1024]{3,2,1,0:T(8,128)S(1)} custom-call(s32[2,4,13]{2,1,0:T(4,128)} %copy-done.3, s32[2,4]{1,0:T(2,128)} %copy-done.4, bf16[2,2,8,128,128]{4,3,2,1,0:T(8,128)(2,1)S(1)} %copy-done.2, bf16[2,2,8,128,128]{4,3,2,1,0:T(8,128)(2,1)S(1)} %collective-permute-done.1.other, ...), custom_call_target="tpu_custom_call" | custom-call | flops 4000000000 | bytes 1048576 | tf_op jit(solution)/shard_map/near_statistics/pallas_call | solution.py:99
  30.5 3.5 %collective-permute-done.5.rest_2_.rest_5_ = bf16[2,2,2,128,128]{4,3,2,1,0:T(8,128)(2,1)S(1)} collective-permute-done((bf16[2,2,2,128,128]{4,3,2,1,0:T(8,128)(2,1)S(1)}, bf16[2,2,2,128,128]{4,3,2,1,0:T(8,128)(2,1)S(1)}, u32[]{:S(2)}, u32[]{:S(2)}) %collective-permute-start.5) | collective-permute-done | bytes 262176 | tf_op jit(solution)/shard_map/ppermute | solution.py:507
  34.1 1.9 %collective-permute-start.7 = (bf16[2,2,2,128,128]{4,3,2,1,0:T(8,128)(2,1)S(1)}, bf16[2,2,2,128,128]{4,3,2,1,0:T(8,128)(2,1)S(1)}, u32[]{:S(2)}, u32[]{:S(2)}) collective-permute-start(bf16[2,2,2,128,128]{4,3,2,1,0:T(8,128)(2,1)S(1)} %collective-permute-done.2.rest_1_.rest_8_), channel_id=1, source_target_pairs={{0,8},{8,16},{16,24},{1,9},{9,17},{17,25},{2,10},{10,18},{18,26},{... | collective-permute-start | bytes 786440 | tf_op jit(solution)/shard_map/ppermute | solution.py:507
  36.0 0.1 collective-permute-start.8
  36.1 0.0 collective-permute-done.6.rest_2_.rest_1_.rest_10_
  36.1 0.8 far_statistics.1.stats_in
  36.9 5.2 %collective-permute-done.7.rest_1_.rest_4_ = bf16[2,2,2,128,128]{4,3,2,1,0:T(8,128)(2,1)S(1)} collective-permute-done((bf16[2,2,2,128,128]{4,3,2,1,0:T(8,128)(2,1)S(1)}, bf16[2,2,2,128,128]{4,3,2,1,0:T(8,128)(2,1)S(1)}, u32[]{:S(2)}, u32[]{:S(2)}) %collective-permute-start.7) | collective-permute-done | bytes 262176 | tf_op jit(solution)/shard_map/ppermute | solution.py:507
  42.1 0.0 collective-permute-done.8.rest_3_.rest_6_
  42.1 14.6 %previous_gradients.1 = (bf16[4,2,2,128,128]{4,3,2,1,0:T(8,128)(2,1)S(1)}, bf16[2,2,2,128,128]{4,3,2,1,0:T(8,128)(2,1)S(1)}, bf16[2,2,2,128,128]{4,3,2,1,0:T(8,1...) custom-call(s32[2,4,13]{2,1,0:T(4,128)} %copy-done.3, s32[2,4]{1,0:T(2,128)} %copy-done.4, ...), custom_call_target="tpu_custom_call" | custom-call | flops 14000000000 | bytes 1048576 | tf_op jit(solution)/shard_map/previous_gradients/pallas_call | solution.py:99
  56.7 0.1 collective-permute-start.9
  56.8 7.7 %collective-permute-start.12 = (bf16[4,2,2,128,128]{4,3,2,1,0:T(8,128)(2,1)S(1)}, bf16[4,2,2,128,128]{4,3,2,1,0:T(8,128)(2,1)S(1)}, u32[]{:S(2)}, u32[]{:S(2)}) collective-permute-start(bf16[4,2,2,128,128]{4,3,2,1,0:T(8,128)(2,1)S(1)} %get-tuple-element.87), channel_id=1, source_target_pairs={{8,0},{16,8},{24,16},{9,1},{17,9},{25,17},{10,2},{18,10},{26,18},{... | collective-permute-start | bytes 1572872 | tf_op jit(solution)/shard_map/ppermute | solution.py:510
  64.5 1.0 far_current_gradients.1
  65.5 0.0 collective-permute-done.9
  65.5 0.1 add_convert_fusion.2
  65.6 0.0 copy-start
  65.6 2.9 %collective-permute-start.10 = (bf16[2,2,2,128,128]{4,3,2,1,0:T(8,128)(2,1)S(1)}, bf16[2,2,2,128,128]{4,3,2,1,0:T(8,128)(2,1)S(1)}, u32[]{:S(2)}, u32[]{:S(2)}) collective-permute-start(bf16[2,2,2,128,128]{4,3,2,1,0:T(8,128)(2,1)S(1)} %add_convert_fusion.2), channel_id=1, source_target_pairs={{8,0},{16,8},{24,16},{9,1},{17,9},{25,17},{10,2},{18,10},{26,18},{... | collective-permute-start | bytes 786440 | tf_op jit(solution)/shard_map/ppermute | solution.py:510
  68.5 1.5 %collective-permute-start.11 = (bf16[2,2,2,128,128]{4,3,2,1,0:T(8,128)(2,1)S(1)}, bf16[2,2,2,128,128]{4,3,2,1,0:T(8,128)(2,1)S(1)}, u32[]{:S(2)}, u32[]{:S(2)}) collective-permute-start(bf16[2,2,2,128,128]{4,3,2,1,0:T(8,128)(2,1)S(1)} %get-tuple-element.78), channel_id=1, source_target_pairs={{0,2},{1,3},{2,0},{3,1},{4,6},{5,7},{6,4},{7,5},{8,10},{9,11},{10,... | collective-permute-start | bytes 786440 | tf_op jit(solution)/shard_map/ppermute | solution.py:501
  70.0 3.8 %near_current_gradients.1 = (f32[2,2,2,128,128]{4,3,2,1,0:T(8,128)S(1)}, f32[2,2,2,128,128]{4,3,2,1,0:T(8,128)S(1)}, bf16[2,4,2,2,128,1024]{5,4,3,2,1,0:T(8,128)(2,1)}) custom-call(s32[2,4,13]{2,1,0:T(4,128)} %copy-done.3, s32[2,4]{1,0:T(2,128)} %copy-done.4, bf16[2,2,8,128,128]{4,3,2,1,0:T(8,128)(2,1)S(1)} %copy-done.2, ...), custom_call_target="tpu_custom_call" | custom-call | flops 6000000000 | bytes 1048576 | tf_op jit(solution)/shard_map/near_current_gradients/pallas_call | solution.py:99
  73.9 2.2 %collective-permute-done.10 = bf16[2,2,2,128,128]{4,3,2,1,0:T(8,128)(2,1)S(1)} collective-permute-done((bf16[2,2,2,128,128]{4,3,2,1,0:T(8,128)(2,1)S(1)}, bf16[2,2,2,128,128]{4,3,2,1,0:T(8,128)(2,1)S(1)}, u32[]{:S(2)}, u32[]{:S(2)}) %collective-permute-start.10) | collective-permute-done | bytes 262176 | tf_op jit(solution)/shard_map/ppermute | solution.py:510
  76.0 0.0 collective-permute-done.11
  76.0 0.1 add_convert_fusion.1
  76.1 0.1 collective-permute-start.16
  76.2 0.0 collective-permute-done.12
  76.2 0.1 add_convert_fusion
  76.3 0.4 collective-permute-start.15
  76.7 0.0 copy-done
  76.7 9.4 %query_results.1 = (bf16[2,128,1024]{2,1,0:T(8,128)(2,1)S(1)}, bf16[2,128,1024]{2,1,0:T(8,128)(2,1)S(1)}, bf16[2,128,1024]{2,1,0:T(8,128)(2,1)S(1)}, bf16[2,128,1024]{2,1,0:T(8,128)(2,1)S(1)}) custom-call(s32[2,4,13]{2,1,0:T(4,128)} %copy-done.3, s32[2,4]{1,0:T(2,128)} %copy-done.4, s32[32]{0:T(128)} %place_ref.6, ...), custom_call_target="tpu_custom_call" | custom-call | flops 20000000000 | bytes 1048576 | tf_op jit(solution)/shard_map/query_results/pallas_call | solution.py:99
  86.1 10.9 %collective-permute-start.13 = (bf16[2,128,1024]{2,1,0:T(8,128)(2,1)S(1)}, bf16[2,128,1024]{2,1,0:T(8,128)(2,1)S(1)}, u32[]{:S(2)}, u32[]{:S(2)}) collective-permute-start(bf16[2,128,1024]{2,1,0:T(8,128)(2,1)S(1)} %get-tuple-element.93), channel_id=1, source_target_pairs={{0,1},{1,0},{2,3},{3,2},{4,5},{5,4},{6,7},{7,6},{8,9},{9,8},{10,11... | collective-permute-start | bytes 1572872 | tf_op jit(solution)/shard_map/ppermute | solution.py:501
  97.0 0.1 collective-permute-start.14
  97.1 0.0 collective-permute-done.16.rest_3_
  97.1 0.0 collective-permute-done.15.rest_2_
  97.1 0.9 key_gradients.1
  98.0 0.5 collective-permute-start.17
  98.5 1.0 collective-permute-done.17.refs_5_
  99.5 0.0 collective-permute-done.13.refs_2_
  99.5 0.0 collective-permute-done.14.refs_3_
  99.5 1.6 %join_halves.1 = (bf16[128,4096]{1,0:T(8,128)(2,1)}, bf16[128,4096]{1,0:T(8,128)(2,1)}, bf16[128,512]{1,0:T(8,128)(2,1)}, bf16[128,512]{1,0:T(8,128)(2,1)}) custom-call(bf16[2,128,1024]{2,1,0:T(8,128)(2,1)S(1)} %get-tuple-element.84.refs_0_, bf16[2,128,1024]{2,1,0:T(8,128)(2,1)S(1)} %get-tuple-element.90.refs_1_, ...), custom_call_target="tpu_custom_call" | custom-call | flops 2000000000 | bytes 1048576 | tf_op jit(solution)/shard_map/join_halves/pallas_call | solution.py:99
  (2 shorter events, 0.0 us)
Async XLA Ops:
  2.5 4.7 %collective-permute-start = (bf16[2,2,128,128]{3,2,1,0:T(8,128)(2,1)S(1)}, bf16[2,2,128,128]{3,2,1,0:T(8,128)(2,1)S(1)}, u32[]{:S(2)}, u32[]{:S(2)}) collective-permute-start(bf16[2,2,128,128]{3,2,1,0:T(8,128)(2,1)S(1)} %get-tuple-element.58), channel_id=1, source_target_pairs={{0,1},{1,0},{2,3},{3,2},{4,5},{5,4},{6,7},{7,6},{8,9},{9,8},{10,11... | collective-permute-start | bytes 393224 | tf_op jit(solution)/shard_map/ppermute | solution.py:501
  6.3 1.0 copy-start.1
  7.2 20.2 %collective-permute-start.1 = (bf16[2,2,8,128,128]{4,3,2,1,0:T(8,128)(2,1)S(1)}, bf16[2,2,8,128,128]{4,3,2,1,0:T(8,128)(2,1)S(1)}, u32[]{:S(2)}, u32[]{:S(2)}) collective-permute-start(bf16[2,2,8,128,128]{4,3,2,1,0:T(8,128)(2,1)S(1)} %get-tuple-element.61), channel_id=1, source_target_pairs={{0,1},{1,0},{2,3},{3,2},{4,5},{5,4},{6,7},{7,6},{8,9},{9,8},{10,11... | collective-permute-start | bytes 3145736 | tf_op jit(solution)/shard_map/ppermute | solution.py:501
  7.3 10.8 %collective-permute-start.3 = (bf16[2,2,2,128,128]{4,3,2,1,0:T(8,128)(2,1)S(1)}, bf16[2,2,2,128,128]{4,3,2,1,0:T(8,128)(2,1)S(1)}, u32[]{:S(2)}, u32[]{:S(2)}) collective-permute-start(bf16[2,2,2,128,128]{4,3,2,1,0:T(8,128)(2,1)S(1)} %pad_maximum_fusion.rest_0_.rest_7_), channel_id=1, source_target_pairs={{0,8},{8,16},{16,24},{1,9},{9,17},{17,25},{2,10},{10,18},{18,26},{... | collective-permute-start | bytes 786440 | tf_op jit(solution)/shard_map/ppermute | solution.py:507
  10.4 12.6 %collective-permute-start.2 = (bf16[2,2,2,128,128]{4,3,2,1,0:T(8,128)(2,1)S(1)}, bf16[2,2,2,128,128]{4,3,2,1,0:T(8,128)(2,1)S(1)}, u32[]{:S(2)}, u32[]{:S(2)}) collective-permute-start(bf16[2,2,2,128,128]{4,3,2,1,0:T(8,128)(2,1)S(1)} %pad_maximum_fusion.rest_0_.rest_7_), channel_id=1, source_target_pairs={{0,2},{1,3},{2,0},{3,1},{4,6},{5,7},{6,4},{7,5},{8,10},{9,11},{10,... | collective-permute-start | bytes 786440 | tf_op jit(solution)/shard_map/ppermute | solution.py:501
  11.8 11.3 %collective-permute-start.4 = (bf16[2,2,2,128,128]{4,3,2,1,0:T(8,128)(2,1)S(1)}, bf16[2,2,2,128,128]{4,3,2,1,0:T(8,128)(2,1)S(1)}, u32[]{:S(2)}, u32[]{:S(2)}) collective-permute-start(bf16[2,2,2,128,128]{4,3,2,1,0:T(8,128)(2,1)S(1)} %pad_maximum_fusion.rest_0_.rest_7_), channel_id=1, source_target_pairs={{0,4},{1,5},{2,6},{3,7},{4,0},{5,1},{6,2},{7,3},{8,12},{9,13},{10,... | collective-permute-start | bytes 786440 | tf_op jit(solution)/shard_map/ppermute | solution.py:501
  17.5 0.6 copy-start.3
  18.1 9.4 %copy-start.4 = (s32[2,4]{1,0:T(2,128)}, s32[2,4]{1,0:T(2,128)S(1)}, u32[]{:S(2)}) copy-start(s32[2,4]{1,0:T(2,128)S(1)} %get-tuple-element.53.counts) | copy-start | bytes 100
  23.0 13.0 %collective-permute-start.6 = (bf16[2,2,2,128,128]{4,3,2,1,0:T(8,128)(2,1)S(1)}, bf16[2,2,2,128,128]{4,3,2,1,0:T(8,128)(2,1)S(1)}, u32[]{:S(2)}, u32[]{:S(2)}) collective-permute-start(bf16[2,2,2,128,128]{4,3,2,1,0:T(8,128)(2,1)S(1)} %collective-permute-done.4.rest_1_.rest_0_.rest_9_), channel_id=1, source_target_pairs={{0,2},{1,3},{2,0},{3,1},{4,6},{5,7},{6,4},{7,5},{8,10},{9,11},{10,... | collective-permute-start | bytes 786440 | tf_op jit(solution)/shard_map/ppermute | solution.py:501
  25.5 8.6 %collective-permute-start.5 = (bf16[2,2,2,128,128]{4,3,2,1,0:T(8,128)(2,1)S(1)}, bf16[2,2,2,128,128]{4,3,2,1,0:T(8,128)(2,1)S(1)}, u32[]{:S(2)}, u32[]{:S(2)}) collective-permute-start(bf16[2,2,2,128,128]{4,3,2,1,0:T(8,128)(2,1)S(1)} %collective-permute-done.4.rest_1_.rest_0_.rest_9_), channel_id=1, source_target_pairs={{0,8},{8,16},{16,24},{1,9},{9,17},{17,25},{2,10},{10,18},{18,26},{... | collective-permute-start | bytes 786440 | tf_op jit(solution)/shard_map/ppermute | solution.py:507
  27.4 1.2 %copy-start.2 = (bf16[2,2,8,128,128]{4,3,2,1,0:T(8,128)(2,1)S(1)}, bf16[2,2,8,128,128]{4,3,2,1,0:T(8,128)(2,1)}, u32[]{:S(2)}) copy-start(bf16[2,2,8,128,128]{4,3,2,1,0:T(8,128)(2,1)} %copy-done.1) | copy-start | bytes 3145732
  34.1 8.0 %collective-permute-start.7 = (bf16[2,2,2,128,128]{4,3,2,1,0:T(8,128)(2,1)S(1)}, bf16[2,2,2,128,128]{4,3,2,1,0:T(8,128)(2,1)S(1)}, u32[]{:S(2)}, u32[]{:S(2)}) collective-permute-start(bf16[2,2,2,128,128]{4,3,2,1,0:T(8,128)(2,1)S(1)} %collective-permute-done.2.rest_1_.rest_8_), channel_id=1, source_target_pairs={{0,8},{8,16},{16,24},{1,9},{9,17},{17,25},{2,10},{10,18},{18,26},{... | collective-permute-start | bytes 786440 | tf_op jit(solution)/shard_map/ppermute | solution.py:507
  36.0 6.1 %collective-permute-start.8 = (bf16[2,2,2,128,128]{4,3,2,1,0:T(8,128)(2,1)S(1)}, bf16[2,2,2,128,128]{4,3,2,1,0:T(8,128)(2,1)S(1)}, u32[]{:S(2)}, u32[]{:S(2)}) collective-permute-start(bf16[2,2,2,128,128]{4,3,2,1,0:T(8,128)(2,1)S(1)} %collective-permute-done.5.rest_2_.rest_5_), channel_id=1, source_target_pairs={{0,2},{1,3},{2,0},{3,1},{4,6},{5,7},{6,4},{7,5},{8,10},{9,11},{10,... | collective-permute-start | bytes 786440 | tf_op jit(solution)/shard_map/ppermute | solution.py:501
  56.7 8.8 %collective-permute-start.9 = (bf16[2,2,2,128,128]{4,3,2,1,0:T(8,128)(2,1)S(1)}, bf16[2,2,2,128,128]{4,3,2,1,0:T(8,128)(2,1)S(1)}, u32[]{:S(2)}, u32[]{:S(2)}) collective-permute-start(bf16[2,2,2,128,128]{4,3,2,1,0:T(8,128)(2,1)S(1)} %get-tuple-element.70), channel_id=1, source_target_pairs={{0,2},{1,3},{2,0},{3,1},{4,6},{5,7},{6,4},{7,5},{8,10},{9,11},{10,... | collective-permute-start | bytes 786440 | tf_op jit(solution)/shard_map/ppermute | solution.py:501
  56.8 19.5 %collective-permute-start.12 = (bf16[4,2,2,128,128]{4,3,2,1,0:T(8,128)(2,1)S(1)}, bf16[4,2,2,128,128]{4,3,2,1,0:T(8,128)(2,1)S(1)}, u32[]{:S(2)}, u32[]{:S(2)}) collective-permute-start(bf16[4,2,2,128,128]{4,3,2,1,0:T(8,128)(2,1)S(1)} %get-tuple-element.87), channel_id=1, source_target_pairs={{8,0},{16,8},{24,16},{9,1},{17,9},{25,17},{10,2},{18,10},{26,18},{... | collective-permute-start | bytes 1572872 | tf_op jit(solution)/shard_map/ppermute | solution.py:510
  65.6 11.1 %copy-start = (f32[320,128]{1,0:T(8,128)S(1)}, f32[320,128]{1,0:T(8,128)}, u32[]{:S(2)}) copy-start(f32[320,128]{1,0:T(8,128)} %constant.2.clone.refs_2_.rest_11_.rest_4_) | copy-start | bytes 491524
  65.6 10.4 %collective-permute-start.10 = (bf16[2,2,2,128,128]{4,3,2,1,0:T(8,128)(2,1)S(1)}, bf16[2,2,2,128,128]{4,3,2,1,0:T(8,128)(2,1)S(1)}, u32[]{:S(2)}, u32[]{:S(2)}) collective-permute-start(bf16[2,2,2,128,128]{4,3,2,1,0:T(8,128)(2,1)S(1)} %add_convert_fusion.2), channel_id=1, source_target_pairs={{8,0},{16,8},{24,16},{9,1},{17,9},{25,17},{10,2},{18,10},{26,18},{... | collective-permute-start | bytes 786440 | tf_op jit(solution)/shard_map/ppermute | solution.py:510
  68.5 7.5 %collective-permute-start.11 = (bf16[2,2,2,128,128]{4,3,2,1,0:T(8,128)(2,1)S(1)}, bf16[2,2,2,128,128]{4,3,2,1,0:T(8,128)(2,1)S(1)}, u32[]{:S(2)}, u32[]{:S(2)}) collective-permute-start(bf16[2,2,2,128,128]{4,3,2,1,0:T(8,128)(2,1)S(1)} %get-tuple-element.78), channel_id=1, source_target_pairs={{0,2},{1,3},{2,0},{3,1},{4,6},{5,7},{6,4},{7,5},{8,10},{9,11},{10,... | collective-permute-start | bytes 786440 | tf_op jit(solution)/shard_map/ppermute | solution.py:501
  76.1 21.0 %collective-permute-start.16 = (bf16[2,2,2,128,128]{4,3,2,1,0:T(8,128)(2,1)S(1)}, bf16[2,2,2,128,128]{4,3,2,1,0:T(8,128)(2,1)S(1)}, u32[]{:S(2)}, u32[]{:S(2)}) collective-permute-start(bf16[2,2,2,128,128]{4,3,2,1,0:T(8,128)(2,1)S(1)} %add_convert_fusion.1), channel_id=1, source_target_pairs={{0,4},{1,5},{2,6},{3,7},{4,0},{5,1},{6,2},{7,3},{8,12},{9,13},{10,... | collective-permute-start | bytes 786440 | tf_op jit(solution)/shard_map/ppermute | solution.py:501
  76.3 20.8 %collective-permute-start.15 = (bf16[2,2,2,128,128]{4,3,2,1,0:T(8,128)(2,1)S(1)}, bf16[2,2,2,128,128]{4,3,2,1,0:T(8,128)(2,1)S(1)}, u32[]{:S(2)}, u32[]{:S(2)}) collective-permute-start(bf16[2,2,2,128,128]{4,3,2,1,0:T(8,128)(2,1)S(1)} %add_convert_fusion), channel_id=1, source_target_pairs={{0,2},{1,3},{2,0},{3,1},{4,6},{5,7},{6,4},{7,5},{8,10},{9,11},{10,... | collective-permute-start | bytes 786440 | tf_op jit(solution)/shard_map/ppermute | solution.py:501
  86.1 13.4 %collective-permute-start.13 = (bf16[2,128,1024]{2,1,0:T(8,128)(2,1)S(1)}, bf16[2,128,1024]{2,1,0:T(8,128)(2,1)S(1)}, u32[]{:S(2)}, u32[]{:S(2)}) collective-permute-start(bf16[2,128,1024]{2,1,0:T(8,128)(2,1)S(1)} %get-tuple-element.93), channel_id=1, source_target_pairs={{0,1},{1,0},{2,3},{3,2},{4,5},{5,4},{6,7},{7,6},{8,9},{9,8},{10,11... | collective-permute-start | bytes 1572872 | tf_op jit(solution)/shard_map/ppermute | solution.py:501
  97.0 2.5 %collective-permute-start.14 = (bf16[2,128,1024]{2,1,0:T(8,128)(2,1)S(1)}, bf16[2,128,1024]{2,1,0:T(8,128)(2,1)S(1)}, u32[]{:S(2)}, u32[]{:S(2)}) collective-permute-start(bf16[2,128,1024]{2,1,0:T(8,128)(2,1)S(1)} %get-tuple-element.94), channel_id=1, source_target_pairs={{0,1},{1,0},{2,3},{3,2},{4,5},{5,4},{6,7},{7,6},{8,9},{9,8},{10,11... | collective-permute-start | bytes 1572872 | tf_op jit(solution)/shard_map/ppermute | solution.py:501
  98.0 1.5 %collective-permute-start.17 = (bf16[2,128,256]{2,1,0:T(8,128)(2,1)S(1)}, bf16[2,128,256]{2,1,0:T(8,128)(2,1)S(1)}, u32[]{:S(2)}, u32[]{:S(2)}) collective-permute-start(bf16[2,128,256]{2,1,0:T(8,128)(2,1)S(1)} %get-tuple-element.99), channel_id=1, source_target_pairs={{0,1},{1,0},{2,3},{3,2},{4,5},{5,4},{6,7},{7,6},{8,9},{9,8},{10,11... | collective-permute-start | bytes 393224 | tf_op jit(solution)/shard_map/ppermute | solution.py:501
where the time goes:
time: 102 us; the launch traced here: 101 us
  Pallas kernels  40.8 us (40%)
  starting transfers between devices  38 us (37%)
  waiting for transfers between devices  16.9 us (17%)
  local copies, waits for them, and re-layouts  4.18 us (4%)
    pallas_call x11, Pallas kernels, run(): pl.pallas_call(kernel, out_shape=[placed(n, a) for n, a in enumerate(outs...  40.8 us
    ppermute x13, starting transfers between devices, cross(): return lax.ppermute(array, 'seq', [(m, m ^ by) for m in range(n_seq)])  20.5 us
    ppermute x2, starting transfers between devices, back(): return lax.ppermute(array, 'grp', [(g + 1, g) for g in range(n_grp - 1)])  10.6 us
    ppermute x3, waiting for transfers between devices, onward(): return lax.ppermute(array, 'grp', [(g, g + 1) for g in range(n_grp - 1)])  8.72 us
    ppermute x3, starting transfers between devices, onward(): return lax.ppermute(array, 'grp', [(g, g + 1) for g in range(n_grp - 1)])  6.94 us
    ppermute x13, waiting for transfers between devices, cross(): return lax.ppermute(array, 'seq', [(m, m ^ by) for m in range(n_seq)])  5.98 us
    unnamed x11, local copies, waits for them, and re-layouts  4.16 us
    ppermute x2, waiting for transfers between devices, back(): return lax.ppermute(array, 'grp', [(g + 1, g) for g in range(n_grp - 1)])  2.17 us
  transfers between devices with their start and end apart: 18, of which 5 were waited for; matrix products, arithmetic and copies ran while one was open for 2% of the time, Pallas kernels for 23%

commit v1 on v0

--- a/solution.py
+++ b/solution.py
@@ -73,11 +73,9 @@
     return math.prod(array.shape) * jnp.dtype(array.dtype).itemsize
 
 
-def call(kernel, out_shape, n_smem, scratch=(), us=1, name=None, n_hbm=0, hbm_out=None, pin=False):
+def call(kernel, out_shape, n_smem, scratch=(), us=1, name=None, n_hbm=0, hbm_out=None, away=None):
     def placed(n, a):
-        if n == hbm_out:
-            return pltpu.HBM(a.shape, a.dtype)
-        return pltpu.VMEM(a.shape, a.dtype) if pin else a
+        return pltpu.HBM(a.shape, a.dtype) if n in (hbm_out, away) else a
 
     def spec(n, a):
         if a.dtype == jnp.int32:
@@ -150,36 +148,40 @@
                 out[1, h, r] = grad[:, columns]
 
 
+FAR_HIGH, FAR_LOW, NEAR_HIGH, NEAR_LOW, ALL = range(5)
+
+
 def make_lists(n_seq, split, key_blocks, key_counts, lists, counts):
     group, member, _ = here(n_seq)
+    bases = (split, 0, n_seq + split, n_seq)
     for i in range(2):
         block = group * n_seq + lax.bitwise_xor(member, i)
-        for section in range(3):
-            counts[i, section] = int(section == 1)
-        lists[i, 1, 0] = i
+        for section in range(4):
+            counts[i, section] = int(section == NEAR_LOW)
+        lists[i, NEAR_LOW, 0] = i
 
         def look(j, _):
             place = lax.bitwise_xor(key_blocks[block, j] - (group - 1) * n_seq, member)
-            section = (place >= n_seq).astype(jnp.int32)
-            section += (place >= n_seq + split).astype(jnp.int32)
+            near = (place >= n_seq).astype(jnp.int32)
+            inner = place - n_seq * near
+            low = (inner < split).astype(jnp.int32)
+            section = 2 * near + low
             n = counts[i, section]
-            lists[i, section, n] = place - jnp.where(section == 0, 0, n_seq) - jnp.where(
-                section == 2, split, 0
-            )
+            lists[i, section, n] = inner - split * (1 - low)
             counts[i, section] = n + 1
             return 0
 
         lax.fori_loop(1, key_counts[block], look, 0)
-        total = 0
-        for section, base in enumerate((0, n_seq, n_seq + split)):
+        total = jnp.int32(0)
+        for section, base in enumerate(bases):
 
             def append(n, m):
-                lists[i, 3, m] = lists[i, section, n] + base
+                lists[i, ALL, m] = lists[i, section, n] + base
                 return m + 1
 
-            total = lax.fori_loop(0, counts[i, section], append, jnp.int32(total))
-        counts[i, 3] = total
-        lists[i, 3, total] = 0
+            total = lax.fori_loop(0, counts[i, section], append, total)
+        counts[i, ALL] = total
+        lists[i, ALL, total] = 0
 
 
 def causal():
@@ -278,7 +280,7 @@
 
 def current_stats(section, lists, counts, own, other, *rest):
     *pieces, stats, store = rest
-    first = section == 1
+    first = section == NEAR_LOW
     if not first:
         stats_in, *pieces = pieces
         stats[...] = stats_in[...]
@@ -295,21 +297,26 @@
 
 
 def previous_grads(n_pieces, lists, counts, own, other, stats_in, *rest):
-    n_ends = 2 * n_pieces - 1
+    n_ends = 2 * n_pieces - 2
     pieces, outs = rest[:n_pieces], rest[n_pieces:n_ends]
-    saved, stats, store, acc, low, sent, kept_scores, kept_dprobs = rest[n_ends:]
-    fill(store, pieces)
+    saved, stats, store, acc, low, sent, kept_scores, kept_dprobs, low_store = rest[n_ends:]
+    fill(low_store, pieces[:2])
+    fill(store, pieces[2:])
     acc[...] = jnp.zeros_like(acc)
     stats[...] = stats_in[...]
     for i, block in enumerate((own, other)):
-        count = counts[i, 0]
+        count = counts[i, FAR_HIGH]
+
+        def look_low(n, _):
+            gather_stats(low_store, lists[i, FAR_LOW, n], block, stats, i, False)
+            return 0
 
         def look(n, _):
-            gather_stats(
-                store, lists[i, 0, n], block, stats, i, False, (n, kept_scores, kept_dprobs)
-            )
-            return 0
-
+            e = lists[i, FAR_HIGH, n]
+            gather_stats(store, e, block, stats, i, False, (n, kept_scores, kept_dprobs))
+            return 0
+
+        lax.fori_loop(0, counts[i, FAR_LOW], look_low, 0)
         lax.fori_loop(0, count, look, 0)
         for h in range(HALF_KV):
             total = stats[i, h, 1:2, :]
@@ -320,7 +327,7 @@
             return pltpu.make_async_copy(low.at[n], saved.at[i, n], sent.at[n])
 
         def add(n, _):
-            e = lists[i, 0, n]
+            e = lists[i, FAR_HIGH, n]
             for h in range(HALF_KV):
                 dk, dv = acc[e, 0, h], acc[e, 1, h]
                 for rows, columns in chunks():
@@ -347,10 +354,9 @@
     write_grads(acc, outs)
 
 
-def current_grads(section, n_pieces, lists, counts, own, other, stats, *rest):
-    pieces, outs = rest[:n_pieces], rest[n_pieces : 2 * n_pieces]
-    saved, store, acc, low, sent = rest[2 * n_pieces :]
-    first = section == 1
+def section_grads(section, n_pieces, lists, counts, own, other, stats, *rest):
+    pieces, (*outs, saved, store, acc, low, sent) = rest[:n_pieces], rest[n_pieces:]
+    first = section == NEAR_LOW
     fill(store, pieces)
     acc[...] = jnp.zeros_like(acc)
     for i, block in enumerate((own, other)):
@@ -392,7 +398,7 @@
 
 
 def query_results(n_seq, lists, counts, place_ref, *rest):
-    n_saved = 3
+    n_saved = 4
     n_pieces = n_seq // CORES
     saved, pieces, rest = rest[:n_saved], rest[n_saved:][: 2 * n_pieces], rest[n_saved + 2 * n_pieces :]
     table, *rest = rest
@@ -443,7 +449,7 @@
                     def _():
                         copy(source, h, i, m, first).wait()
 
-            found = [lists[i, 3, m] for m in pair]
+            found = [lists[i, ALL, m] for m in pair]
             keys_t = jnp.concatenate([store[e, 0, h].T for e in found], axis=1)
             values_t = jnp.concatenate([store[e, 1, h].T for e in found], axis=1)
             for _, columns in chunks():
@@ -522,23 +528,23 @@
     lists, counts = call(
         functools.partial(make_lists, n_seq, split),
         (
-            jax.ShapeDtypeStruct((2, 4, n_listed + 1), jnp.int32),
-            jax.ShapeDtypeStruct((2, 4), jnp.int32),
+            jax.ShapeDtypeStruct((2, 5, n_listed + 1), jnp.int32),
+            jax.ShapeDtypeStruct((2, 5), jnp.int32),
         ),
         2, us=2, name="block_lists",
     )(key_blocks, key_counts)
 
-    def prepared(kernel, shape, first, second, name):
+    def prepared(kernel, shape, first, second, name, away=None):
         held = [pltpu.VMEM(a.shape, a.dtype) for a in (first, second, table)]
         return call(
             functools.partial(kernel, n_seq), (shape, shape), 1,
-            [*held, pltpu.SemaphoreType.DMA((3,))], us=1, name=name, n_hbm=3, pin=True,
+            [*held, pltpu.SemaphoreType.DMA((3,))], us=1, name=name, n_hbm=3, away=away,
         )(block_position, first, second, table)
 
     kv_keep, kv_send = prepared(prepare_kv, kv_shape, key_input, value_input, "rotate_keys")
     kv_got = cross(kv_send, 1)
     query_late, kv_keep = lax.optimization_barrier((query_input, kv_keep))
-    q_keep, q_send = prepared(prepare_queries, q_shape, query_late, out_grad, "rotate_queries")
+    q_keep, q_send = prepared(prepare_queries, q_shape, query_late, out_grad, "rotate_queries", 0)
     q_send, q_keep, kv_got, kv_keep = lax.optimization_barrier((q_send, q_keep, kv_got, kv_keep))
     q_got = cross(q_send, 1)
     near = [jnp.stack([kv_keep, kv_got])]
@@ -550,7 +556,7 @@
         near += [piece_k, along(piece_k, 1)]
         far += [onward(piece_k), None]
     stats = call(
-        functools.partial(current_stats, 1), stats_shape, 2, [pltpu.VMEM((split, *piece), BF16)],
+        functools.partial(current_stats, NEAR_LOW), stats_shape, 2, [pltpu.VMEM((split, *piece), BF16)],
         us=4, name="near_statistics",
     )(lists, counts, q_keep, q_got, *near[:2])
     ready, far[2], stats = lax.optimization_barrier((ready, far[2], stats))
@@ -558,7 +564,7 @@
     for k in range(2, n_pieces, 2):
         far[k + 1] = along(far[k], 1)
     stats = call(
-        functools.partial(current_stats, 2), stats_shape, 2,
+        functools.partial(current_stats, NEAR_HIGH), stats_shape, 2,
         [pltpu.VMEM((n_seq - split, *piece), BF16)], us=4, name="far_statistics",
     )(lists, counts, q_keep, q_got, stats, *near[2:])
 
@@ -574,18 +580,19 @@
             us=us, name=name, hbm_out=len(outs),
         )
 
-    kept = pltpu.VMEM((n_far, HALF_KV, BLK, ROWS), F32)
-    two = jax.ShapeDtypeStruct((2 * CORES, *piece), BF16)
-    first_far, *far_grads, far_saved, stats = grads_call(
-        functools.partial(previous_grads, n_pieces), n_far, n_seq, (two,) + (low,) * (n_pieces - 2),
-        14, "previous_gradients", (kept, kept), (stats_shape,),
+    n_high = n_seq - split
+    kept = pltpu.VMEM((min(n_high, n_listed - 1), HALF_KV, BLK, ROWS), F32)
+    *far_grads, far_high_saved, stats = grads_call(
+        functools.partial(previous_grads, n_pieces), min(n_high, n_listed - 1), n_high,
+        (low,) * (n_pieces - 2), 14, "previous_gradients",
+        (kept, kept, pltpu.VMEM((split, *piece), BF16)), (stats_shape,),
     )(lists, counts, q_keep, q_got, stats, *far)
 
-    def current_call(section, outs, name, pieces, after):
+    def section_call(section, outs, name, pieces, after):
         stats_late, _ = lax.optimization_barrier((stats, after))
         n_store = CORES * len(pieces)
         *grads, saved = grads_call(
-            functools.partial(current_grads, section, len(pieces)), min(n_store, n_listed), n_store,
+            functools.partial(section_grads, section, len(pieces)), min(n_store, n_listed), n_store,
             outs, 6, name,
         )(lists, counts, q_keep, q_got, stats_late, *pieces)
         return grads, saved
@@ -593,26 +600,28 @@
     def total(*terms):
         return sum(term.astype(F32) for term in terms).astype(BF16)
 
-    from_far = back(first_far)
     crossing = [along(grad, 1) for grad in far_grads[1::2]]
-    high_grads, high_saved = current_call(
-        2, [high, low] * (n_pieces // 2 - 1), "far_current_gradients", near[2:], far_grads[0]
+    high_grads, near_high_saved = section_call(
+        NEAR_HIGH, [high, low] * (n_pieces // 2 - 1), "current_high_gradients", near[2:],
+        far_grads[0],
     )
     crossing, high_grads = lax.optimization_barrier((crossing, high_grads))
-    arrived = [
-        back(total(grad, extra)) for grad, extra in zip(far_grads[0::2], crossing)
-    ]
+    arrived = [back(total(grad, extra)) for grad, extra in zip(far_grads[0::2], crossing)]
     swapped = [along(grad, 1) for grad in high_grads[1::2]]
-    low_grads, low_saved = current_call(
-        1, [high, high], "near_current_gradients", near[:2], high_grads[0]
+    first_far, far_low_saved = section_call(
+        FAR_LOW, [low, low], "previous_low_gradients", far[:2], high_grads[0]
     )
-    low_grads, from_far = lax.optimization_barrier((low_grads, from_far))
-    from_next = along(total(low_grads[1], from_far[CORES:]), 1)
-    merged = [
-        total(*terms) for terms in zip(high_grads[0::2], arrived, swapped)
-    ]
+    arrived, swapped, first_far = lax.optimization_barrier((arrived, swapped, first_far))
+    merged = [total(*terms) for terms in zip(high_grads[0::2], arrived, swapped)]
+    second = back(first_far[1])
+    low_grads, near_low_saved = section_call(
+        NEAR_LOW, [high, high], "current_low_gradients", near[:2], merged
+    )
+    low_grads, second = lax.optimization_barrier((low_grads, second))
+    next_part = total(low_grads[1], second)
+    first, next_part = lax.optimization_barrier((first_far[0], next_part))
     half_out = jax.ShapeDtypeStruct((2, BLK, RATIO * HEAD_DIM), BF16)
-    place_late, _ = lax.optimization_barrier((block_position, merged))
+    place_late, _ = lax.optimization_barrier((block_position, next_part))
     wide = pltpu.VMEM((HEAD_DIM, ROWS), F32)
     slots = (HALF_KV, 2, n_listed + 1)
     halves = call(
@@ -621,12 +630,12 @@
             pltpu.VMEM((2 * n_seq, *piece), BF16), pltpu.VMEM((*slots, 2, BLK, ROWS), BF16),
             wide, wide, pltpu.SemaphoreType.DMA(slots),
         ],
-        us=20, name="query_results", n_hbm=3,
-    )(lists, counts, place_late, far_saved, low_saved, high_saved, *far, *near, table)
+        us=20, name="query_results", n_hbm=4,
+    )(lists, counts, place_late, far_high_saved, far_low_saved, near_high_saved, near_low_saved, *far, *near, table)
     own_halves, other_halves = halves[:HALF_KV], halves[HALF_KV:]
     other_halves = lax.optimization_barrier(list(other_halves))
     got_halves = [cross(half, 1) for half in other_halves]
-    final = [low_grads[0], from_far[:CORES], from_next]
+    final = [low_grads[0], back(first), along(next_part, 1)]
     final += [along(part, 2 + 2 * n) for n, part in enumerate(merged)]
     own_halves = list(own_halves)
     final[0], own_halves[1] = lax.optimization_barrier((final[0], own_halves[1]))

time: 102 us -> 108 us (1.059)
  starting transfers between devices: 38 us -> 44.1 us
  waiting for transfers between devices: 16.9 us -> 18.1 us
  Pallas kernels: 40.8 us -> 39.6 us
    ppermute x13, starting transfers between devices: 20.5 us -> 30.8 us  [cross(): return lax.ppermute(array, 'seq', [(m, m ^ by) for m in range(n_seq)])]
    ppermute x2 -> x3, starting transfers between devices: 10.6 us -> 6.36 us  [back(): return lax.ppermute(array, 'grp', [(g + 1, g) for g in range(n_grp - 1)])]
    ppermute x13, waiting for transfers between devices: 5.98 us -> 9.15 us  [cross(): return lax.ppermute(array, 'seq', [(m, m ^ by) for m in range(n_seq)])]
    ppermute x2 -> x3, waiting for transfers between devices: 2.17 us -> 0.83 us  [back(): return lax.ppermute(array, 'grp', [(g + 1, g) for g in range(n_grp - 1)])]
    pallas_call x11 -> x12, Pallas kernels: 40.8 us -> 39.6 us  [run(): pl.pallas_call(kernel, out_shape=[placed(n, a) for n, a in enumerate(outs...]
    unnamed x11 -> x9, local copies, waits for them, and re-layouts: 4.16 us -> 3.2 us
  transfers between devices with their start and end apart: 18 -> 19, of which waited for: 5 -> 7; matrix products, arithmetic and copies ran while one was open for 2% -> 1% of each run, Pallas kernels for 23% -> 27%
where the time goes in v1:
time: 108 us; the launch traced here: 106 us
  starting transfers between devices  44.1 us (41%)
  Pallas kernels  39.6 us (37%)
  waiting for transfers between devices  18.1 us (17%)
  local copies, waits for them, and re-layouts  3.2 us (3%)
    pallas_call x12, Pallas kernels, run(): pl.pallas_call(kernel, out_shape=[placed(n, a) for n, a in enumerate(outs...  39.6 us
    ppermute x13, starting transfers between devices, cross(): return lax.ppermute(array, 'seq', [(m, m ^ by) for m in range(n_seq)])  30.8 us
    ppermute x13, waiting for transfers between devices, cross(): return lax.ppermute(array, 'seq', [(m, m ^ by) for m in range(n_seq)])  9.15 us
    ppermute x3, waiting for transfers between devices, onward(): return lax.ppermute(array, 'grp', [(g, g + 1) for g in range(n_grp - 1)])  8.07 us
    ppermute x3, starting transfers between devices, onward(): return lax.ppermute(array, 'grp', [(g, g + 1) for g in range(n_grp - 1)])  6.94 us
    ppermute x3, starting transfers between devices, back(): return lax.ppermute(array, 'grp', [(g + 1, g) for g in range(n_grp - 1)])  6.36 us
    unnamed x9, local copies, waits for them, and re-layouts  3.2 us
  transfers between devices with their start and end apart: 19, of which 7 were waited for; matrix products, arithmetic and copies ran while one was open for 1% of the time, Pallas kernels for 27%

profile of v1, /device:TPU:5, one launch (start us, length us, event | category | flops | bytes accessed | tf_op | source)
XLA Modules:
  0.0 106.1 jit_solution(7381401118914367915)
XLA Ops:
  0.6 1.9 %rotate_keys.1 = (bf16[2,2,128,128]{3,2,1,0:T(8,128)(2,1)S(1)}, bf16[2,2,128,128]{3,2,1,0:T(8,128)(2,1)S(1)}) custom-call(s32[32]{0:T(128)} %place_ref.6, bf16[128,512]{1,0:T(8,128)(2,1)} %refs_0_.1, bf16[128,512]{1,0:T(8,128)(2,1)} %refs_1_.2, f32[320,128]{1,0:T(8,128)} %constant.2.clone.refs_2_.rest_12_.rest_4_), custom_call_target="tpu_custom_call" | custom-call | flops 1000000000 | bytes 1048576 | tf_op jit(solution)/shard_map/rotate_keys/pallas_call | solution.py:97
  2.5 0.7 collective-permute-start
  3.2 3.8 %rotate_queries.1 = (bf16[2,2,8,128,128]{4,3,2,1,0:T(8,128)(2,1)}, bf16[2,2,8,128,128]{4,3,2,1,0:T(8,128)(2,1)S(1)}) custom-call(s32[32]{0:T(128)} %place_ref.6, bf16[128,4096]{1,0:T(8,128)(2,1)} %refs_0_.2, bf16[128,4096]{1,0:T(8,128)(2,1)} %refs_1_.3, f32[320,128]{1,0:T(8,128)} %constant.2.clone.refs_2_.rest_12_.rest_4_), custom_call_target="tpu_custom_call" | custom-call | flops 1000000000 | bytes 1048576 | tf_op jit(solution)/shard_map/rotate_queries/pallas_call | solution.py:97
  7.1 0.0 collective-permute-done
  7.1 0.1 collective-permute-start.1
  7.2 3.1 %collective-permute-start.3 = (bf16[2,2,2,128,128]{4,3,2,1,0:T(8,128)(2,1)S(1)}, bf16[2,2,2,128,128]{4,3,2,1,0:T(8,128)(2,1)S(1)}, u32[]{:S(2)}, u32[]{:S(2)}) collective-permute-start(bf16[2,2,2,128,128]{4,3,2,1,0:T(8,128)(2,1)S(1)} %pad_maximum_fusion.rest_0_.rest_8_), channel_id=1, source_target_pairs={{0,8},{8,16},{16,24},{1,9},{9,17},{17,25},{2,10},{10,18},{18,26},{... | collective-permute-start | bytes 786440 | tf_op jit(solution)/shard_map/ppermute | solution.py:513
  10.3 1.4 %collective-permute-start.2 = (bf16[2,2,2,128,128]{4,3,2,1,0:T(8,128)(2,1)S(1)}, bf16[2,2,2,128,128]{4,3,2,1,0:T(8,128)(2,1)S(1)}, u32[]{:S(2)}, u32[]{:S(2)}) collective-permute-start(bf16[2,2,2,128,128]{4,3,2,1,0:T(8,128)(2,1)S(1)} %pad_maximum_fusion.rest_0_.rest_8_), channel_id=1, source_target_pairs={{0,2},{1,3},{2,0},{3,1},{4,6},{5,7},{6,4},{7,5},{8,10},{9,11},{10,... | collective-permute-start | bytes 786440 | tf_op jit(solution)/shard_map/ppermute | solution.py:507
  11.7 2.3 %collective-permute-start.4 = (bf16[2,2,2,128,128]{4,3,2,1,0:T(8,128)(2,1)S(1)}, bf16[2,2,2,128,128]{4,3,2,1,0:T(8,128)(2,1)S(1)}, u32[]{:S(2)}, u32[]{:S(2)}) collective-permute-start(bf16[2,2,2,128,128]{4,3,2,1,0:T(8,128)(2,1)S(1)} %pad_maximum_fusion.rest_0_.rest_8_), channel_id=1, source_target_pairs={{0,4},{1,5},{2,6},{3,7},{4,0},{5,1},{6,2},{7,3},{8,12},{9,13},{10,... | collective-permute-start | bytes 786440 | tf_op jit(solution)/shard_map/ppermute | solution.py:507
  14.0 1.4 %copy.12.key_blocks = s32[32,12]{1,0:T(8,128)} copy(s32[32,12]{0,1:T(8,128)} %param.12) | data formatting | bytes 3072 | tf_op args[4]
  15.4 2.0 %block_lists.1 = (s32[2,5,13]{2,1,0:T(8,128)S(1)}, s32[2,5]{1,0:T(2,128)S(1)}) custom-call(s32[32,12]{1,0:T(8,128)} %copy.12.key_blocks, s32[32]{0:T(128)} %key_counts.1), custom_call_target="tpu_custom_call" | custom-call | flops 2000000000 | bytes 1048576 | tf_op jit(solution)/shard_map/block_lists/pallas_call | solution.py:97
  17.4 0.0 copy-start.2
  17.4 0.6 copy-done.2
  18.0 0.0 copy-start.3
  18.0 0.0 collective-permute-done.3.rest_0_.rest_4_
  18.0 5.0 %collective-permute-done.2.rest_1_.rest_9_ = bf16[2,2,2,128,128]{4,3,2,1,0:T(8,128)(2,1)S(1)} collective-permute-done((bf16[2,2,2,128,128]{4,3,2,1,0:T(8,128)(2,1)S(1)}, bf16[2,2,2,128,128]{4,3,2,1,0:T(8,128)(2,1)S(1)}, u32[]{:S(2)}, u32[]{:S(2)}) %collective-permute-start.2) | collective-permute-done | bytes 262176 | tf_op jit(solution)/shard_map/ppermute | solution.py:507
  23.0 0.0 collective-permute-done.4.rest_1_.rest_0_.rest_10_
  23.0 2.5 %collective-permute-start.6 = (bf16[2,2,2,128,128]{4,3,2,1,0:T(8,128)(2,1)S(1)}, bf16[2,2,2,128,128]{4,3,2,1,0:T(8,128)(2,1)S(1)}, u32[]{:S(2)}, u32[]{:S(2)}) collective-permute-start(bf16[2,2,2,128,128]{4,3,2,1,0:T(8,128)(2,1)S(1)} %collective-permute-done.4.rest_1_.rest_0_.rest_10_), channel_id=1, source_target_pairs={{0,2},{1,3},{2,0},{3,1},{4,6},{5,7},{6,4},{7,5},{8,10},{9,11},{10,... | collective-permute-start | bytes 786440 | tf_op jit(solution)/shard_map/ppermute | solution.py:507
  25.4 1.9 %collective-permute-start.5 = (bf16[2,2,2,128,128]{4,3,2,1,0:T(8,128)(2,1)S(1)}, bf16[2,2,2,128,128]{4,3,2,1,0:T(8,128)(2,1)S(1)}, u32[]{:S(2)}, u32[]{:S(2)}) collective-permute-start(bf16[2,2,2,128,128]{4,3,2,1,0:T(8,128)(2,1)S(1)} %collective-permute-done.4.rest_1_.rest_0_.rest_10_), channel_id=1, source_target_pairs={{0,8},{8,16},{16,24},{1,9},{9,17},{17,25},{2,10},{10,18},{18,26},{... | collective-permute-start | bytes 786440 | tf_op jit(solution)/shard_map/ppermute | solution.py:513
  27.3 0.0 collective-permute-done.1.other
  27.4 0.0 copy-done.3
  27.4 0.0 copy-start.1
  27.4 1.2 %copy-done.1 = bf16[2,2,8,128,128]{4,3,2,1,0:T(8,128)(2,1)S(1)} copy-done((bf16[2,2,8,128,128]{4,3,2,1,0:T(8,128)(2,1)S(1)}, bf16[2,2,8,128,128]{4,3,2,1,0:T(8,128)(2,1)}, u32[]{:S(2)}) %copy-start.1) | copy-done | bytes 1048600
  28.6 2.5 %near_statistics.1.rest_0_ = f32[2,2,8,1024]{3,2,1,0:T(8,128)S(1)} custom-call(s32[2,5,13]{2,1,0:T(8,128)} %copy-done.2, s32[2,5]{1,0:T(2,128)} %copy-done.3, bf16[2,2,8,128,128]{4,3,2,1,0:T(8,128)(2,1)S(1)} %copy-done.1, bf16[2,2,8,128,128]{4,3,2,1,0:T(8,128)(2,1)S(1)} %collective-permute-done.1.other, ...), custom_call_target="tpu_custom_call" | custom-call | flops 4000000000 | bytes 1048576 | tf_op jit(solution)/shard_map/near_statistics/pallas_call | solution.py:97
  31.1 3.0 %collective-permute-done.5.rest_2_.rest_6_ = bf16[2,2,2,128,128]{4,3,2,1,0:T(8,128)(2,1)S(1)} collective-permute-done((bf16[2,2,2,128,128]{4,3,2,1,0:T(8,128)(2,1)S(1)}, bf16[2,2,2,128,128]{4,3,2,1,0:T(8,128)(2,1)S(1)}, u32[]{:S(2)}, u32[]{:S(2)}) %collective-permute-start.5) | collective-permute-done | bytes 262176 | tf_op jit(solution)/shard_map/ppermute | solution.py:513
  34.0 1.9 %collective-permute-start.7 = (bf16[2,2,2,128,128]{4,3,2,1,0:T(8,128)(2,1)S(1)}, bf16[2,2,2,128,128]{4,3,2,1,0:T(8,128)(2,1)S(1)}, u32[]{:S(2)}, u32[]{:S(2)}) collective-permute-start(bf16[2,2,2,128,128]{4,3,2,1,0:T(8,128)(2,1)S(1)} %collective-permute-done.2.rest_1_.rest_9_), channel_id=1, source_target_pairs={{0,8},{8,16},{16,24},{1,9},{9,17},{17,25},{2,10},{10,18},{18,26},{... | collective-permute-start | bytes 786440 | tf_op jit(solution)/shard_map/ppermute | solution.py:513
  35.9 0.1 collective-permute-start.8
  36.0 0.0 collective-permute-done.6.rest_2_.rest_1_.rest_11_
  36.0 0.9 far_statistics.1.stats_in
  36.9 5.1 %collective-permute-done.7.rest_1_.rest_5_ = bf16[2,2,2,128,128]{4,3,2,1,0:T(8,128)(2,1)S(1)} collective-permute-done((bf16[2,2,2,128,128]{4,3,2,1,0:T(8,128)(2,1)S(1)}, bf16[2,2,2,128,128]{4,3,2,1,0:T(8,128)(2,1)S(1)}, u32[]{:S(2)}, u32[]{:S(2)}) %collective-permute-start.7) | collective-permute-done | bytes 262176 | tf_op jit(solution)/shard_map/ppermute | solution.py:513
  42.0 0.0 collective-permute-done.8.rest_3_.rest_7_
  42.0 7.9 %previous_gradients.1 = (bf16[2,2,2,128,128]{4,3,2,1,0:T(8,128)(2,1)S(1)}, bf16[2,2,2,128,128]{4,3,2,1,0:T(8,128)(2,1)S(1)}, bf16[2,4,2,2,128,1024]{5,4,3,2,1,0:T(8,128)(2,1)}, f32[2,2,8,1024]{3,2,1,0:T(8,128)S(1)}) custom-call(s32[2,5,13]{2,1,0:T(8,128)} %copy-done.2, s32[2,5]{1,0:T(2,128)} %copy-done.3, bf16[2,2,8,128,128]{4,3,2,1,0:T(8,128)(2,1)S(1)} %copy-done.1, ...), custom_call_target="tpu_custom_call" | custom-call | flops 14000000000 | bytes 1048576 | tf_op jit(solution)/shard_map/previous_gradients/pallas_call | solution.py:97
  50.0 4.8 %collective-permute-start.9 = (bf16[2,2,2,128,128]{4,3,2,1,0:T(8,128)(2,1)S(1)}, bf16[2,2,2,128,128]{4,3,2,1,0:T(8,128)(2,1)S(1)}, u32[]{:S(2)}, u32[]{:S(2)}) collective-permute-start(bf16[2,2,2,128,128]{4,3,2,1,0:T(8,128)(2,1)S(1)} %get-tuple-element.80), channel_id=1, source_target_pairs={{0,2},{1,3},{2,0},{3,1},{4,6},{5,7},{6,4},{7,5},{8,10},{9,11},{10,... | collective-permute-start | bytes 786440 | tf_op jit(solution)/shard_map/ppermute | solution.py:507
  54.8 1.1 current_high_gradients.1
  55.8 2.7 %collective-permute-done.9 = bf16[2,2,2,128,128]{4,3,2,1,0:T(8,128)(2,1)S(1)} collective-permute-done((bf16[2,2,2,128,128]{4,3,2,1,0:T(8,128)(2,1)S(1)}, bf16[2,2,2,128,128]{4,3,2,1,0:T(8,128)(2,1)S(1)}, u32[]{:S(2)}, u32[]{:S(2)}) %collective-permute-start.9) | collective-permute-done | bytes 262176 | tf_op jit(solution)/shard_map/ppermute | solution.py:507
  58.5 0.1 add_convert_fusion.2
  58.6 1.9 %collective-permute-start.10 = (bf16[2,2,2,128,128]{4,3,2,1,0:T(8,128)(2,1)S(1)}, bf16[2,2,2,128,128]{4,3,2,1,0:T(8,128)(2,1)S(1)}, u32[]{:S(2)}, u32[]{:S(2)}) collective-permute-start(bf16[2,2,2,128,128]{4,3,2,1,0:T(8,128)(2,1)S(1)} %add_convert_fusion.2), channel_id=1, source_target_pairs={{8,0},{16,8},{24,16},{9,1},{17,9},{25,17},{10,2},{18,10},{26,18},{... | collective-permute-start | bytes 786440 | tf_op jit(solution)/shard_map/ppermute | solution.py:516
  60.6 1.5 %collective-permute-start.11 = (bf16[2,2,2,128,128]{4,3,2,1,0:T(8,128)(2,1)S(1)}, bf16[2,2,2,128,128]{4,3,2,1,0:T(8,128)(2,1)S(1)}, u32[]{:S(2)}, u32[]{:S(2)}) collective-permute-start(bf16[2,2,2,128,128]{4,3,2,1,0:T(8,128)(2,1)S(1)} %get-tuple-element.86), channel_id=1, source_target_pairs={{0,2},{1,3},{2,0},{3,1},{4,6},{5,7},{6,4},{7,5},{8,10},{9,11},{10,... | collective-permute-start | bytes 786440 | tf_op jit(solution)/shard_map/ppermute | solution.py:507
  62.1 4.7 %previous_low_gradients.1 = (bf16[2,2,2,128,128]{4,3,2,1,0:T(8,128)(2,1)S(1)}, bf16[2,2,2,128,128]{4,3,2,1,0:T(8,128)(2,1)S(1)}, bf16[2,4,2,2,128,1024]{5,4,3,2,1,0:T(8,128)(2,1)}) custom-call(s32[2,5,13]{2,1,0:T(8,128)} %copy-done.2, s32[2,5]{1,0:T(2,128)} %copy-done.3, bf16[2,2,8,128,128]{4,3,2,1,0:T(8,128)(2,1)S(1)} %copy-done.1, ...), custom_call_target="tpu_custom_call" | custom-call | flops 6000000000 | bytes 1048576 | tf_op jit(solution)/shard_map/previous_low_gradients/pallas_call | solution.py:97
  66.8 0.0 collective-permute-done.10
  66.8 0.4 collective-permute-done.11
  67.3 0.1 add_convert_fusion.1
  67.4 0.0 copy-start
  67.4 3.0 %collective-permute-start.17 = (bf16[2,2,2,128,128]{4,3,2,1,0:T(8,128)(2,1)S(1)}, bf16[2,2,2,128,128]{4,3,2,1,0:T(8,128)(2,1)S(1)}, u32[]{:S(2)}, u32[]{:S(2)}) collective-permute-start(bf16[2,2,2,128,128]{4,3,2,1,0:T(8,128)(2,1)S(1)} %add_convert_fusion.1), channel_id=1, source_target_pairs={{0,4},{1,5},{2,6},{3,7},{4,0},{5,1},{6,2},{7,3},{8,12},{9,13},{10,... | collective-permute-start | bytes 786440 | tf_op jit(solution)/shard_map/ppermute | solution.py:507
  70.3 1.9 %collective-permute-start.12 = (bf16[2,2,2,128,128]{4,3,2,1,0:T(8,128)(2,1)S(1)}, bf16[2,2,2,128,128]{4,3,2,1,0:T(8,128)(2,1)S(1)}, u32[]{:S(2)}, u32[]{:S(2)}) collective-permute-start(bf16[2,2,2,128,128]{4,3,2,1,0:T(8,128)(2,1)S(1)} %get-tuple-element.97), channel_id=1, source_target_pairs={{8,0},{16,8},{24,16},{9,1},{17,9},{25,17},{10,2},{18,10},{26,18},{... | collective-permute-start | bytes 786440 | tf_op jit(solution)/shard_map/ppermute | solution.py:516
  72.3 4.4 %current_low_gradients.1 = (f32[2,2,2,128,128]{4,3,2,1,0:T(8,128)S(1)}, f32[2,2,2,128,128]{4,3,2,1,0:T(8,128)S(1)}, bf16[2,4,2,2,128,1024]{5,4,3,2,1,0:T(8,128)(2,1)}) custom-call(s32[2,5,13]{2,1,0:T(8,128)} %copy-done.2, s32[2,5]{1,0:T(2,128)} %copy-done.3, bf16[2,2,8,128,128]{4,3,2,1,0:T(8,128)(2,1)S(1)} %copy-done.1, ...), custom_call_target="tpu_custom_call" | custom-call | flops 6000000000 | bytes 1048576 | tf_op jit(solution)/shard_map/current_low_gradients/pallas_call | solution.py:97
  76.6 0.8 collective-permute-done.12
  77.4 0.1 add_convert_fusion
  77.5 1.7 %collective-permute-start.16 = (bf16[2,2,2,128,128]{4,3,2,1,0:T(8,128)(2,1)S(1)}, bf16[2,2,2,128,128]{4,3,2,1,0:T(8,128)(2,1)S(1)}, u32[]{:S(2)}, u32[]{:S(2)}) collective-permute-start(bf16[2,2,2,128,128]{4,3,2,1,0:T(8,128)(2,1)S(1)} %add_convert_fusion), channel_id=1, source_target_pairs={{0,2},{1,3},{2,0},{3,1},{4,6},{5,7},{6,4},{7,5},{8,10},{9,11},{10,... | collective-permute-start | bytes 786440 | tf_op jit(solution)/shard_map/ppermute | solution.py:507
  79.2 2.5 %collective-permute-start.15 = (bf16[2,2,2,128,128]{4,3,2,1,0:T(8,128)(2,1)S(1)}, bf16[2,2,2,128,128]{4,3,2,1,0:T(8,128)(2,1)S(1)}, u32[]{:S(2)}, u32[]{:S(2)}) collective-permute-start(bf16[2,2,2,128,128]{4,3,2,1,0:T(8,128)(2,1)S(1)} %get-tuple-element.115), channel_id=1, source_target_pairs={{8,0},{16,8},{24,16},{9,1},{17,9},{25,17},{10,2},{18,10},{26,18},{... | collective-permute-start | bytes 786440 | tf_op jit(solution)/shard_map/ppermute | solution.py:516
  81.7 0.0 copy-done
  81.7 8.1 %query_results.1 = (bf16[2,128,1024]{2,1,0:T(8,128)(2,1)S(1)}, bf16[2,128,1024]{2,1,0:T(8,128)(2,1)S(1)}, bf16[2,128,1024]{2,1,0:T(8,128)(2,1)S(1)}, bf16[2,128,1024]{2,1,0:T(8,128)(2,1)S(1)}) custom-call(s32[2,5,13]{2,1,0:T(8,128)} %copy-done.2, s32[2,5]{1,0:T(2,128)} %copy-done.3, s32[32]{0:T(128)} %place_ref.6, ...), custom_call_target="tpu_custom_call" | custom-call | flops 20000000000 | bytes 1048576 | tf_op jit(solution)/shard_map/query_results/pallas_call | solution.py:97
  89.8 12.3 %collective-permute-start.13 = (bf16[2,128,1024]{2,1,0:T(8,128)(2,1)S(1)}, bf16[2,128,1024]{2,1,0:T(8,128)(2,1)S(1)}, u32[]{:S(2)}, u32[]{:S(2)}) collective-permute-start(bf16[2,128,1024]{2,1,0:T(8,128)(2,1)S(1)} %get-tuple-element.112), channel_id=1, source_target_pairs={{0,1},{1,0},{2,3},{3,2},{4,5},{5,4},{6,7},{7,6},{8,9},{9,8},{10,11... | collective-permute-start | bytes 1572872 | tf_op jit(solution)/shard_map/ppermute | solution.py:507
  102.0 0.1 collective-permute-start.14
  102.1 0.0 collective-permute-done.17.rest_3_
  102.1 0.0 collective-permute-done.15.rest_1_
  102.1 0.0 collective-permute-done.16.rest_2_
  102.1 0.9 key_gradients.1
  103.0 0.5 collective-permute-start.18
  103.5 1.0 collective-permute-done.18.refs_5_
  104.5 0.0 collective-permute-done.13.refs_2_
  104.5 0.0 collective-permute-done.14.refs_3_
  104.5 1.6 %join_halves.1 = (bf16[128,4096]{1,0:T(8,128)(2,1)}, bf16[128,4096]{1,0:T(8,128)(2,1)}, bf16[128,512]{1,0:T(8,128)(2,1)}, bf16[128,512]{1,0:T(8,128)(2,1)}) custom-call(bf16[2,128,1024]{2,1,0:T(8,128)(2,1)S(1)} %get-tuple-element.106.refs_0_, bf16[2,128,1024]{2,1,0:T(8,128)(2,1)S(1)} %get-tuple-element.109.refs_1_, ...), custom_call_target="tpu_custom_call" | custom-call | flops 2000000000 | bytes 1048576 | tf_op jit(solution)/shard_map/join_halves/pallas_call | solution.py:97
  (1 shorter events, 0.0 us)
Async XLA Ops:
  2.5 4.6 %collective-permute-start = (bf16[2,2,128,128]{3,2,1,0:T(8,128)(2,1)S(1)}, bf16[2,2,128,128]{3,2,1,0:T(8,128)(2,1)S(1)}, u32[]{:S(2)}, u32[]{:S(2)}) collective-permute-start(bf16[2,2,128,128]{3,2,1,0:T(8,128)(2,1)S(1)} %get-tuple-element.67), channel_id=1, source_target_pairs={{0,1},{1,0},{2,3},{3,2},{4,5},{5,4},{6,7},{7,6},{8,9},{9,8},{10,11... | collective-permute-start | bytes 393224 | tf_op jit(solution)/shard_map/ppermute | solution.py:507
  7.1 20.3 %collective-permute-start.1 = (bf16[2,2,8,128,128]{4,3,2,1,0:T(8,128)(2,1)S(1)}, bf16[2,2,8,128,128]{4,3,2,1,0:T(8,128)(2,1)S(1)}, u32[]{:S(2)}, u32[]{:S(2)}) collective-permute-start(bf16[2,2,8,128,128]{4,3,2,1,0:T(8,128)(2,1)S(1)} %get-tuple-element.70), channel_id=1, source_target_pairs={{0,1},{1,0},{2,3},{3,2},{4,5},{5,4},{6,7},{7,6},{8,9},{9,8},{10,11... | collective-permute-start | bytes 3145736 | tf_op jit(solution)/shard_map/ppermute | solution.py:507
  7.2 10.8 %collective-permute-start.3 = (bf16[2,2,2,128,128]{4,3,2,1,0:T(8,128)(2,1)S(1)}, bf16[2,2,2,128,128]{4,3,2,1,0:T(8,128)(2,1)S(1)}, u32[]{:S(2)}, u32[]{:S(2)}) collective-permute-start(bf16[2,2,2,128,128]{4,3,2,1,0:T(8,128)(2,1)S(1)} %pad_maximum_fusion.rest_0_.rest_8_), channel_id=1, source_target_pairs={{0,8},{8,16},{16,24},{1,9},{9,17},{17,25},{2,10},{10,18},{18,26},{... | collective-permute-start | bytes 786440 | tf_op jit(solution)/shard_map/ppermute | solution.py:513
  10.3 12.6 %collective-permute-start.2 = (bf16[2,2,2,128,128]{4,3,2,1,0:T(8,128)(2,1)S(1)}, bf16[2,2,2,128,128]{4,3,2,1,0:T(8,128)(2,1)S(1)}, u32[]{:S(2)}, u32[]{:S(2)}) collective-permute-start(bf16[2,2,2,128,128]{4,3,2,1,0:T(8,128)(2,1)S(1)} %pad_maximum_fusion.rest_0_.rest_8_), channel_id=1, source_target_pairs={{0,2},{1,3},{2,0},{3,1},{4,6},{5,7},{6,4},{7,5},{8,10},{9,11},{10,... | collective-permute-start | bytes 786440 | tf_op jit(solution)/shard_map/ppermute | solution.py:507
  11.7 11.3 %collective-permute-start.4 = (bf16[2,2,2,128,128]{4,3,2,1,0:T(8,128)(2,1)S(1)}, bf16[2,2,2,128,128]{4,3,2,1,0:T(8,128)(2,1)S(1)}, u32[]{:S(2)}, u32[]{:S(2)}) collective-permute-start(bf16[2,2,2,128,128]{4,3,2,1,0:T(8,128)(2,1)S(1)} %pad_maximum_fusion.rest_0_.rest_8_), channel_id=1, source_target_pairs={{0,4},{1,5},{2,6},{3,7},{4,0},{5,1},{6,2},{7,3},{8,12},{9,13},{10,... | collective-permute-start | bytes 786440 | tf_op jit(solution)/shard_map/ppermute | solution.py:507
  17.4 0.6 copy-start.2
  18.0 9.4 %copy-start.3 = (s32[2,5]{1,0:T(2,128)}, s32[2,5]{1,0:T(2,128)S(1)}, u32[]{:S(2)}) copy-start(s32[2,5]{1,0:T(2,128)S(1)} %get-tuple-element.62.counts) | copy-start | bytes 124
  23.0 13.1 %collective-permute-start.6 = (bf16[2,2,2,128,128]{4,3,2,1,0:T(8,128)(2,1)S(1)}, bf16[2,2,2,128,128]{4,3,2,1,0:T(8,128)(2,1)S(1)}, u32[]{:S(2)}, u32[]{:S(2)}) collective-permute-start(bf16[2,2,2,128,128]{4,3,2,1,0:T(8,128)(2,1)S(1)} %collective-permute-done.4.rest_1_.rest_0_.rest_10_), channel_id=1, source_target_pairs={{0,2},{1,3},{2,0},{3,1},{4,6},{5,7},{6,4},{7,5},{8,10},{9,11},{10,... | collective-permute-start | bytes 786440 | tf_op jit(solution)/shard_map/ppermute | solution.py:507
  25.4 8.6 %collective-permute-start.5 = (bf16[2,2,2,128,128]{4,3,2,1,0:T(8,128)(2,1)S(1)}, bf16[2,2,2,128,128]{4,3,2,1,0:T(8,128)(2,1)S(1)}, u32[]{:S(2)}, u32[]{:S(2)}) collective-permute-start(bf16[2,2,2,128,128]{4,3,2,1,0:T(8,128)(2,1)S(1)} %collective-permute-done.4.rest_1_.rest_0_.rest_10_), channel_id=1, source_target_pairs={{0,8},{8,16},{16,24},{1,9},{9,17},{17,25},{2,10},{10,18},{18,26},{... | collective-permute-start | bytes 786440 | tf_op jit(solution)/shard_map/ppermute | solution.py:513
  27.4 1.2 %copy-start.1 = (bf16[2,2,8,128,128]{4,3,2,1,0:T(8,128)(2,1)S(1)}, bf16[2,2,8,128,128]{4,3,2,1,0:T(8,128)(2,1)}, u32[]{:S(2)}) copy-start(bf16[2,2,8,128,128]{4,3,2,1,0:T(8,128)(2,1)} %get-tuple-element.69.own) | copy-start | bytes 3145732
  34.0 8.0 %collective-permute-start.7 = (bf16[2,2,2,128,128]{4,3,2,1,0:T(8,128)(2,1)S(1)}, bf16[2,2,2,128,128]{4,3,2,1,0:T(8,128)(2,1)S(1)}, u32[]{:S(2)}, u32[]{:S(2)}) collective-permute-start(bf16[2,2,2,128,128]{4,3,2,1,0:T(8,128)(2,1)S(1)} %collective-permute-done.2.rest_1_.rest_9_), channel_id=1, source_target_pairs={{0,8},{8,16},{16,24},{1,9},{9,17},{17,25},{2,10},{10,18},{18,26},{... | collective-permute-start | bytes 786440 | tf_op jit(solution)/shard_map/ppermute | solution.py:513
  35.9 6.1 %collective-permute-start.8 = (bf16[2,2,2,128,128]{4,3,2,1,0:T(8,128)(2,1)S(1)}, bf16[2,2,2,128,128]{4,3,2,1,0:T(8,128)(2,1)S(1)}, u32[]{:S(2)}, u32[]{:S(2)}) collective-permute-start(bf16[2,2,2,128,128]{4,3,2,1,0:T(8,128)(2,1)S(1)} %collective-permute-done.5.rest_2_.rest_6_), channel_id=1, source_target_pairs={{0,2},{1,3},{2,0},{3,1},{4,6},{5,7},{6,4},{7,5},{8,10},{9,11},{10,... | collective-permute-start | bytes 786440 | tf_op jit(solution)/shard_map/ppermute | solution.py:507
  50.0 8.6 %collective-permute-start.9 = (bf16[2,2,2,128,128]{4,3,2,1,0:T(8,128)(2,1)S(1)}, bf16[2,2,2,128,128]{4,3,2,1,0:T(8,128)(2,1)S(1)}, u32[]{:S(2)}, u32[]{:S(2)}) collective-permute-start(bf16[2,2,2,128,128]{4,3,2,1,0:T(8,128)(2,1)S(1)} %get-tuple-element.80), channel_id=1, source_target_pairs={{0,2},{1,3},{2,0},{3,1},{4,6},{5,7},{6,4},{7,5},{8,10},{9,11},{10,... | collective-permute-start | bytes 786440 | tf_op jit(solution)/shard_map/ppermute | solution.py:507
  58.6 8.2 %collective-permute-start.10 = (bf16[2,2,2,128,128]{4,3,2,1,0:T(8,128)(2,1)S(1)}, bf16[2,2,2,128,128]{4,3,2,1,0:T(8,128)(2,1)S(1)}, u32[]{:S(2)}, u32[]{:S(2)}) collective-permute-start(bf16[2,2,2,128,128]{4,3,2,1,0:T(8,128)(2,1)S(1)} %add_convert_fusion.2), channel_id=1, source_target_pairs={{8,0},{16,8},{24,16},{9,1},{17,9},{25,17},{10,2},{18,10},{26,18},{... | collective-permute-start | bytes 786440 | tf_op jit(solution)/shard_map/ppermute | solution.py:516
  60.6 6.7 %collective-permute-start.11 = (bf16[2,2,2,128,128]{4,3,2,1,0:T(8,128)(2,1)S(1)}, bf16[2,2,2,128,128]{4,3,2,1,0:T(8,128)(2,1)S(1)}, u32[]{:S(2)}, u32[]{:S(2)}) collective-permute-start(bf16[2,2,2,128,128]{4,3,2,1,0:T(8,128)(2,1)S(1)} %get-tuple-element.86), channel_id=1, source_target_pairs={{0,2},{1,3},{2,0},{3,1},{4,6},{5,7},{6,4},{7,5},{8,10},{9,11},{10,... | collective-permute-start | bytes 786440 | tf_op jit(solution)/shard_map/ppermute | solution.py:507
  67.4 14.3 %copy-start = (f32[320,128]{1,0:T(8,128)S(1)}, f32[320,128]{1,0:T(8,128)}, u32[]{:S(2)}) copy-start(f32[320,128]{1,0:T(8,128)} %constant.2.clone.refs_2_.rest_12_.rest_4_) | copy-start | bytes 491524
  67.4 34.8 %collective-permute-start.17 = (bf16[2,2,2,128,128]{4,3,2,1,0:T(8,128)(2,1)S(1)}, bf16[2,2,2,128,128]{4,3,2,1,0:T(8,128)(2,1)S(1)}, u32[]{:S(2)}, u32[]{:S(2)}) collective-permute-start(bf16[2,2,2,128,128]{4,3,2,1,0:T(8,128)(2,1)S(1)} %add_convert_fusion.1), channel_id=1, source_target_pairs={{0,4},{1,5},{2,6},{3,7},{4,0},{5,1},{6,2},{7,3},{8,12},{9,13},{10,... | collective-permute-start | bytes 786440 | tf_op jit(solution)/shard_map/ppermute | solution.py:507
  70.3 7.1 %collective-permute-start.12 = (bf16[2,2,2,128,128]{4,3,2,1,0:T(8,128)(2,1)S(1)}, bf16[2,2,2,128,128]{4,3,2,1,0:T(8,128)(2,1)S(1)}, u32[]{:S(2)}, u32[]{:S(2)}) collective-permute-start(bf16[2,2,2,128,128]{4,3,2,1,0:T(8,128)(2,1)S(1)} %get-tuple-element.97), channel_id=1, source_target_pairs={{8,0},{16,8},{24,16},{9,1},{17,9},{25,17},{10,2},{18,10},{26,18},{... | collective-permute-start | bytes 786440 | tf_op jit(solution)/shard_map/ppermute | solution.py:516
  77.5 24.6 %collective-permute-start.16 = (bf16[2,2,2,128,128]{4,3,2,1,0:T(8,128)(2,1)S(1)}, bf16[2,2,2,128,128]{4,3,2,1,0:T(8,128)(2,1)S(1)}, u32[]{:S(2)}, u32[]{:S(2)}) collective-permute-start(bf16[2,2,2,128,128]{4,3,2,1,0:T(8,128)(2,1)S(1)} %add_convert_fusion), channel_id=1, source_target_pairs={{0,2},{1,3},{2,0},{3,1},{4,6},{5,7},{6,4},{7,5},{8,10},{9,11},{10,... | collective-permute-start | bytes 786440 | tf_op jit(solution)/shard_map/ppermute | solution.py:507
  79.2 23.0 %collective-permute-start.15 = (bf16[2,2,2,128,128]{4,3,2,1,0:T(8,128)(2,1)S(1)}, bf16[2,2,2,128,128]{4,3,2,1,0:T(8,128)(2,1)S(1)}, u32[]{:S(2)}, u32[]{:S(2)}) collective-permute-start(bf16[2,2,2,128,128]{4,3,2,1,0:T(8,128)(2,1)S(1)} %get-tuple-element.115), channel_id=1, source_target_pairs={{8,0},{16,8},{24,16},{9,1},{17,9},{25,17},{10,2},{18,10},{26,18},{... | collective-permute-start | bytes 786440 | tf_op jit(solution)/shard_map/ppermute | solution.py:516
  89.8 14.7 %collective-permute-start.13 = (bf16[2,128,1024]{2,1,0:T(8,128)(2,1)S(1)}, bf16[2,128,1024]{2,1,0:T(8,128)(2,1)S(1)}, u32[]{:S(2)}, u32[]{:S(2)}) collective-permute-start(bf16[2,128,1024]{2,1,0:T(8,128)(2,1)S(1)} %get-tuple-element.112), channel_id=1, source_target_pairs={{0,1},{1,0},{2,3},{3,2},{4,5},{5,4},{6,7},{7,6},{8,9},{9,8},{10,11... | collective-permute-start | bytes 1572872 | tf_op jit(solution)/shard_map/ppermute | solution.py:507
  102.0 2.5 %collective-permute-start.14 = (bf16[2,128,1024]{2,1,0:T(8,128)(2,1)S(1)}, bf16[2,128,1024]{2,1,0:T(8,128)(2,1)S(1)}, u32[]{:S(2)}, u32[]{:S(2)}) collective-permute-start(bf16[2,128,1024]{2,1,0:T(8,128)(2,1)S(1)} %get-tuple-element.113), channel_id=1, source_target_pairs={{0,1},{1,0},{2,3},{3,2},{4,5},{5,4},{6,7},{7,6},{8,9},{9,8},{10,11... | collective-permute-start | bytes 1572872 | tf_op jit(solution)/shard_map/ppermute | solution.py:507
  103.0 1.5 %collective-permute-start.18 = (bf16[2,128,256]{2,1,0:T(8,128)(2,1)S(1)}, bf16[2,128,256]{2,1,0:T(8,128)(2,1)S(1)}, u32[]{:S(2)}, u32[]{:S(2)}) collective-permute-start(bf16[2,128,256]{2,1,0:T(8,128)(2,1)S(1)} %get-tuple-element.117), channel_id=1, source_target_pairs={{0,1},{1,0},{2,3},{3,2},{4,5},{5,4},{6,7},{7,6},{8,9},{9,8},{10,11... | collective-permute-start | bytes 393224 | tf_op jit(solution)/shard_map/ppermute | solution.py:507

commit v2 on v0

--- a/solution.py
+++ b/solution.py
@@ -216,15 +216,16 @@
     for h in range(HALF_KV):
         for rows, columns in chunks():
             scores, dprobs = pair_scores(store, e, h, block, rows, diagonal)
-            if kept is not None:
-                n, kept_scores, kept_dprobs = kept
-                kept_scores[n, h, :, columns] = scores
-                kept_dprobs[n, h, :, columns] = dprobs
             top = jnp.max(scores, axis=0, keepdims=True)
             if not diagonal:
                 old_top = stats[i, h, 0:1, columns]
                 top = jnp.maximum(top, old_top)
             weights = jnp.exp2((scores - top) * TO_LOG2)
+            if kept is not None:
+                n, kept_weights, kept_dprobs, tops = kept
+                kept_weights[n, h, :, columns] = weights
+                kept_dprobs[n, h, :, columns] = dprobs
+                tops[n, h, 0:1, columns] = top * TO_LOG2
             total = jnp.sum(weights, axis=0, keepdims=True)
             mixed = jnp.sum(weights * dprobs, axis=0, keepdims=True)
             if not diagonal:
@@ -297,7 +298,7 @@
 def previous_grads(n_pieces, lists, counts, own, other, stats_in, *rest):
     n_ends = 2 * n_pieces - 1
     pieces, outs = rest[:n_pieces], rest[n_pieces:n_ends]
-    saved, stats, store, acc, low, sent, kept_scores, kept_dprobs = rest[n_ends:]
+    saved, stats, store, acc, low, sent, kept_weights, kept_dprobs, tops = rest[n_ends:]
     fill(store, pieces)
     acc[...] = jnp.zeros_like(acc)
     stats[...] = stats_in[...]
@@ -305,9 +306,8 @@
         count = counts[i, 0]
 
         def look(n, _):
-            gather_stats(
-                store, lists[i, 0, n], block, stats, i, False, (n, kept_scores, kept_dprobs)
-            )
+            kept = (n, kept_weights, kept_dprobs, tops)
+            gather_stats(store, lists[i, 0, n], block, stats, i, False, kept)
             return 0
 
         lax.fori_loop(0, count, look, 0)
@@ -324,9 +324,8 @@
             for h in range(HALF_KV):
                 dk, dv = acc[e, 0, h], acc[e, 1, h]
                 for rows, columns in chunks():
-                    probs = jnp.exp2(
-                        kept_scores[n, h, :, columns] * TO_LOG2 - stats[i, h, 0:1, columns]
-                    )
+                    share = jnp.exp2(tops[n, h, 0:1, columns] - stats[i, h, 0:1, columns])
+                    probs = kept_weights[n, h, :, columns] * share
                     dscores = probs * (kept_dprobs[n, h, :, columns] - stats[i, h, 2:3, columns])
                     probs, dscores = probs.astype(BF16), dscores.astype(BF16)
                     low[n, h, 0, :, columns] = probs
@@ -532,23 +531,24 @@
         held = [pltpu.VMEM(a.shape, a.dtype) for a in (first, second, table)]
         return call(
             functools.partial(kernel, n_seq), (shape, shape), 1,
-            [*held, pltpu.SemaphoreType.DMA((3,))], us=1, name=name, n_hbm=3, pin=True,
+            [*held, pltpu.SemaphoreType.DMA((3,))], us=1, name=name, n_hbm=3,
         )(block_position, first, second, table)
 
     kv_keep, kv_send = prepared(prepare_kv, kv_shape, key_input, value_input, "rotate_keys")
     kv_got = cross(kv_send, 1)
-    query_late, kv_keep = lax.optimization_barrier((query_input, kv_keep))
-    q_keep, q_send = prepared(prepare_queries, q_shape, query_late, out_grad, "rotate_queries")
-    q_send, q_keep, kv_got, kv_keep = lax.optimization_barrier((q_send, q_keep, kv_got, kv_keep))
-    q_got = cross(q_send, 1)
     near = [jnp.stack([kv_keep, kv_got])]
     near.append(along(near[0], 1))
     ready, first_far = lax.optimization_barrier((near[1], onward(near[0])))
+    query_late, _ = lax.optimization_barrier((query_input, near[0]))
+    q_keep, q_send = prepared(prepare_queries, q_shape, query_late, out_grad, "rotate_queries")
     far = [first_far, None]
     for k in range(2, n_pieces, 2):
-        piece_k, _ = lax.optimization_barrier((along(near[0], k), ready))
+        piece_k, q_send, lists, counts, _ = lax.optimization_barrier(
+            (along(near[0], k), q_send, lists, counts, ready)
+        )
         near += [piece_k, along(piece_k, 1)]
         far += [onward(piece_k), None]
+    q_got = cross(q_send, 1)
     stats = call(
         functools.partial(current_stats, 1), stats_shape, 2, [pltpu.VMEM((split, *piece), BF16)],
         us=4, name="near_statistics",
@@ -578,7 +578,7 @@
     two = jax.ShapeDtypeStruct((2 * CORES, *piece), BF16)
     first_far, *far_grads, far_saved, stats = grads_call(
         functools.partial(previous_grads, n_pieces), n_far, n_seq, (two,) + (low,) * (n_pieces - 2),
-        14, "previous_gradients", (kept, kept), (stats_shape,),
+        14, "previous_gradients", (kept, kept, pltpu.VMEM((n_far, HALF_KV, 8, ROWS), F32)), (stats_shape,),
     )(lists, counts, q_keep, q_got, stats, *far)
 
     def current_call(section, outs, name, pieces, after):

time: 102 us -> 101 us (level)
  starting transfers between devices: 38 us -> 26 us
  waiting for transfers between devices: 16.9 us -> 25.6 us
  Pallas kernels: 40.8 us -> 45.8 us
  local copies, waits for them, and re-layouts: 4.18 us -> 1.99 us
    ppermute x2, starting transfers between devices: 10.6 us -> 3.97 us  [back(): return lax.ppermute(array, 'grp', [(g + 1, g) for g in range(n_grp - 1)])]
    ppermute x13, starting transfers between devices: 20.5 us -> 15.1 us  [cross(): return lax.ppermute(array, 'seq', [(m, m ^ by) for m in range(n_seq)])]
    pallas_call x11, Pallas kernels: 40.8 us -> 45.8 us  [run(): pl.pallas_call(kernel, out_shape=[placed(n, a) for n, a in enumerate(outs...]
    ppermute x2, waiting for transfers between devices: 2.17 us -> 6.38 us  [back(): return lax.ppermute(array, 'grp', [(g + 1, g) for g in range(n_grp - 1)])]
    ppermute x3, waiting for transfers between devices: 8.72 us -> 11.3 us  [onward(): return lax.ppermute(array, 'grp', [(g, g + 1) for g in range(n_grp - 1)])]
    unnamed x11 -> x7, local copies, waits for them, and re-layouts: 4.16 us -> 1.98 us
    ppermute x13, waiting for transfers between devices: 5.98 us -> 7.97 us  [cross(): return lax.ppermute(array, 'seq', [(m, m ^ by) for m in range(n_seq)])]
  transfers between devices with their start and end apart: 18 -> 18, of which waited for: 5 -> 7; matrix products, arithmetic and copies ran while one was open for 2% -> 2% of each run, Pallas kernels for 23% -> 24%
where the time goes in v2:
time: 101 us
  Pallas kernels  45.8 us (45%)
  starting transfers between devices  26 us (26%)
  waiting for transfers between devices  25.6 us (25%)
  local copies, waits for them, and re-layouts  1.99 us (2%)
    pallas_call x11, Pallas kernels, run(): pl.pallas_call(kernel, out_shape=[placed(n, a) for n, a in enumerate(outs...  45.8 us
    ppermute x13, starting transfers between devices, cross(): return lax.ppermute(array, 'seq', [(m, m ^ by) for m in range(n_seq)])  15.1 us
    ppermute x3, waiting for transfers between devices, onward(): return lax.ppermute(array, 'grp', [(g, g + 1) for g in range(n_grp - 1)])  11.3 us
    ppermute x13, waiting for transfers between devices, cross(): return lax.ppermute(array, 'seq', [(m, m ^ by) for m in range(n_seq)])  7.97 us
    ppermute x3, starting transfers between devices, onward(): return lax.ppermute(array, 'grp', [(g, g + 1) for g in range(n_grp - 1)])  6.94 us
    ppermute x2, waiting for transfers between devices, back(): return lax.ppermute(array, 'grp', [(g + 1, g) for g in range(n_grp - 1)])  6.38 us
    ppermute x2, starting transfers between devices, back(): return lax.ppermute(array, 'grp', [(g + 1, g) for g in range(n_grp - 1)])  3.97 us
  transfers between devices with their start and end apart: 18, of which 7 were waited for; matrix products, arithmetic and copies ran while one was open for 2% of the time, Pallas kernels for 24%

profile of v2, /device:TPU:5, one launch (start us, length us, event | category | flops | bytes accessed | tf_op | source)
XLA Modules:
  0.0 100.6 jit_solution(5734455946250785884)
XLA Ops:
  0.6 1.9 %rotate_keys.1 = (bf16[2,2,128,128]{3,2,1,0:T(8,128)(2,1)S(1)}, bf16[2,2,128,128]{3,2,1,0:T(8,128)(2,1)S(1)}) custom-call(s32[32]{0:T(128)} %place_ref.6, bf16[128,512]{1,0:T(8,128)(2,1)} %refs_0_.1, bf16[128,512]{1,0:T(8,128)(2,1)} %refs_1_.2, f32[320,128]{1,0:T(8,128)} %constant.2.clone.refs_2_.rest_11_.rest_4_), custom_call_target="tpu_custom_call" | custom-call | flops 1000000000 | bytes 1048576 | tf_op jit(solution)/shard_map/rotate_keys/pallas_call | solution.py:99
  2.5 0.7 collective-permute-start
  3.2 1.4 %copy.12.key_blocks = s32[32,12]{1,0:T(8,128)} copy(s32[32,12]{0,1:T(8,128)} %param.12) | data formatting | bytes 3072 | tf_op args[4]
  4.6 0.0 collective-permute-done
  4.7 3.1 %collective-permute-start.3 = (bf16[2,2,2,128,128]{4,3,2,1,0:T(8,128)(2,1)S(1)}, bf16[2,2,2,128,128]{4,3,2,1,0:T(8,128)(2,1)S(1)}, u32[]{:S(2)}, u32[]{:S(2)}) collective-permute-start(bf16[2,2,2,128,128]{4,3,2,1,0:T(8,128)(2,1)S(1)} %pad_maximum_fusion.rest_0_.rest_7_), channel_id=1, source_target_pairs={{0,8},{8,16},{16,24},{1,9},{9,17},{17,25},{2,10},{10,18},{18,26},{... | collective-permute-start | bytes 786440 | tf_op jit(solution)/shard_map/ppermute | solution.py:506
  7.8 1.4 %collective-permute-start.2 = (bf16[2,2,2,128,128]{4,3,2,1,0:T(8,128)(2,1)S(1)}, bf16[2,2,2,128,128]{4,3,2,1,0:T(8,128)(2,1)S(1)}, u32[]{:S(2)}, u32[]{:S(2)}) collective-permute-start(bf16[2,2,2,128,128]{4,3,2,1,0:T(8,128)(2,1)S(1)} %pad_maximum_fusion.rest_0_.rest_7_), channel_id=1, source_target_pairs={{0,2},{1,3},{2,0},{3,1},{4,6},{5,7},{6,4},{7,5},{8,10},{9,11},{10,... | collective-permute-start | bytes 786440 | tf_op jit(solution)/shard_map/ppermute | solution.py:500
  9.1 2.3 %collective-permute-start.1 = (bf16[2,2,2,128,128]{4,3,2,1,0:T(8,128)(2,1)S(1)}, bf16[2,2,2,128,128]{4,3,2,1,0:T(8,128)(2,1)S(1)}, u32[]{:S(2)}, u32[]{:S(2)}) collective-permute-start(bf16[2,2,2,128,128]{4,3,2,1,0:T(8,128)(2,1)S(1)} %pad_maximum_fusion.rest_0_.rest_7_), channel_id=1, source_target_pairs={{0,4},{1,5},{2,6},{3,7},{4,0},{5,1},{6,2},{7,3},{8,12},{9,13},{10,... | collective-permute-start | bytes 786440 | tf_op jit(solution)/shard_map/ppermute | solution.py:500
  11.4 2.1 %block_lists.1 = (s32[2,4,13]{2,1,0:T(4,128)S(1)}, s32[2,4]{1,0:T(2,128)S(1)}) custom-call(s32[32,12]{1,0:T(8,128)} %copy.12.key_blocks, s32[32]{0:T(128)} %key_counts.1), custom_call_target="tpu_custom_call" | custom-call | flops 2000000000 | bytes 1048576 | tf_op jit(solution)/shard_map/block_lists/pallas_call | solution.py:99
  13.5 0.0 copy-start.1
  13.6 0.6 copy-done.1
  14.1 0.0 copy-start.2
  14.1 3.0 %rotate_queries.1 = (bf16[2,2,8,128,128]{4,3,2,1,0:T(8,128)(2,1)S(1)}, bf16[2,2,8,128,128]{4,3,2,1,0:T(8,128)(2,1)S(1)}) custom-call(s32[32]{0:T(128)} %place_ref.6, bf16[128,4096]{1,0:T(8,128)(2,1)} %refs_0_.2, bf16[128,4096]{1,0:T(8,128)(2,1)} %refs_1_.3, f32[320,128]{1,0:T(8,128)} %constant.2.clone.refs_2_.rest_11_.rest_4_), custom_call_target="tpu_custom_call" | custom-call | flops 1000000000 | bytes 1048576 | tf_op jit(solution)/shard_map/rotate_queries/pallas_call | solution.py:99
  17.2 0.0 collective-permute-done.3.rest_0_.rest_3_
  17.2 3.8 %collective-permute-done.2.rest_1_.rest_8_ = bf16[2,2,2,128,128]{4,3,2,1,0:T(8,128)(2,1)S(1)} collective-permute-done((bf16[2,2,2,128,128]{4,3,2,1,0:T(8,128)(2,1)S(1)}, bf16[2,2,2,128,128]{4,3,2,1,0:T(8,128)(2,1)S(1)}, u32[]{:S(2)}, u32[]{:S(2)}) %collective-permute-start.2) | collective-permute-done | bytes 262176 | tf_op jit(solution)/shard_map/ppermute | solution.py:500
  21.0 0.0 collective-permute-done.1.rest_1_.rest_0_.rest_9_
  21.0 3.5 %collective-permute-start.4 = (bf16[2,2,8,128,128]{4,3,2,1,0:T(8,128)(2,1)S(1)}, bf16[2,2,8,128,128]{4,3,2,1,0:T(8,128)(2,1)S(1)}, u32[]{:S(2)}, u32[]{:S(2)}) collective-permute-start(bf16[2,2,8,128,128]{4,3,2,1,0:T(8,128)(2,1)S(1)} %get-tuple-element.60), channel_id=1, source_target_pairs={{0,1},{1,0},{2,3},{3,2},{4,5},{5,4},{6,7},{7,6},{8,9},{9,8},{10,11... | collective-permute-start | bytes 3145736 | tf_op jit(solution)/shard_map/ppermute | solution.py:500
  24.4 0.2 collective-permute-start.6
  24.6 1.9 %collective-permute-start.5 = (bf16[2,2,2,128,128]{4,3,2,1,0:T(8,128)(2,1)S(1)}, bf16[2,2,2,128,128]{4,3,2,1,0:T(8,128)(2,1)S(1)}, u32[]{:S(2)}, u32[]{:S(2)}) collective-permute-start(bf16[2,2,2,128,128]{4,3,2,1,0:T(8,128)(2,1)S(1)} %collective-permute-done.1.rest_1_.rest_0_.rest_9_), channel_id=1, source_target_pairs={{0,8},{8,16},{16,24},{1,9},{9,17},{17,25},{2,10},{10,18},{18,26},{... | collective-permute-start | bytes 786440 | tf_op jit(solution)/shard_map/ppermute | solution.py:506
  26.5 0.2 collective-permute-done.4.other
  26.7 0.0 copy-done.2
  26.7 2.4 %near_statistics.1.rest_0_ = f32[2,2,8,1024]{3,2,1,0:T(8,128)S(1)} custom-call(s32[2,4,13]{2,1,0:T(4,128)} %copy-done.1, s32[2,4]{1,0:T(2,128)} %copy-done.2, bf16[2,2,8,128,128]{4,3,2,1,0:T(8,128)(2,1)S(1)} %get-tuple-element.59.own, bf16[2,2,8,128,128]{4,3,2,1,0:T(8,128)(2,1)S(1)} %collective-permute-done.4.other, ...), custom_call_target="tpu_custom_call" | custom-call | flops 4000000000 | bytes 1048576 | tf_op jit(solution)/shard_map/near_statistics/pallas_call | solution.py:99
  29.1 5.9 %collective-permute-done.5.rest_2_.rest_5_ = bf16[2,2,2,128,128]{4,3,2,1,0:T(8,128)(2,1)S(1)} collective-permute-done((bf16[2,2,2,128,128]{4,3,2,1,0:T(8,128)(2,1)S(1)}, bf16[2,2,2,128,128]{4,3,2,1,0:T(8,128)(2,1)S(1)}, u32[]{:S(2)}, u32[]{:S(2)}) %collective-permute-start.5) | collective-permute-done | bytes 262176 | tf_op jit(solution)/shard_map/ppermute | solution.py:506
  35.0 1.9 %collective-permute-start.7 = (bf16[2,2,2,128,128]{4,3,2,1,0:T(8,128)(2,1)S(1)}, bf16[2,2,2,128,128]{4,3,2,1,0:T(8,128)(2,1)S(1)}, u32[]{:S(2)}, u32[]{:S(2)}) collective-permute-start(bf16[2,2,2,128,128]{4,3,2,1,0:T(8,128)(2,1)S(1)} %collective-permute-done.2.rest_1_.rest_8_), channel_id=1, source_target_pairs={{0,8},{8,16},{16,24},{1,9},{9,17},{17,25},{2,10},{10,18},{18,26},{... | collective-permute-start | bytes 786440 | tf_op jit(solution)/shard_map/ppermute | solution.py:506
  36.9 1.4 %collective-permute-start.8 = (bf16[2,2,2,128,128]{4,3,2,1,0:T(8,128)(2,1)S(1)}, bf16[2,2,2,128,128]{4,3,2,1,0:T(8,128)(2,1)S(1)}, u32[]{:S(2)}, u32[]{:S(2)}) collective-permute-start(bf16[2,2,2,128,128]{4,3,2,1,0:T(8,128)(2,1)S(1)} %collective-permute-done.5.rest_2_.rest_5_), channel_id=1, source_target_pairs={{0,2},{1,3},{2,0},{3,1},{4,6},{5,7},{6,4},{7,5},{8,10},{9,11},{10,... | collective-permute-start | bytes 786440 | tf_op jit(solution)/shard_map/ppermute | solution.py:500
  38.3 0.0 collective-permute-done.6.rest_2_.rest_1_.rest_10_
  38.3 0.8 far_statistics.1.stats_in
  39.1 5.4 %collective-permute-done.7.rest_1_.rest_4_ = bf16[2,2,2,128,128]{4,3,2,1,0:T(8,128)(2,1)S(1)} collective-permute-done((bf16[2,2,2,128,128]{4,3,2,1,0:T(8,128)(2,1)S(1)}, bf16[2,2,2,128,128]{4,3,2,1,0:T(8,128)(2,1)S(1)}, u32[]{:S(2)}, u32[]{:S(2)}) %collective-permute-start.7) | collective-permute-done | bytes 262176 | tf_op jit(solution)/shard_map/ppermute | solution.py:506
  44.5 0.0 collective-permute-done.8.rest_3_.rest_6_
  44.5 17.9 %previous_gradients.1 = (bf16[4,2,2,128,128]{4,3,2,1,0:T(8,128)(2,1)S(1)}, bf16[2,2,2,128,128]{4,3,2,1,0:T(8,128)(2,1)S(1)}, bf16[2,2,2,128,128]{4,3,2,1,0:T(8,1...) custom-call(s32[2,4,13]{2,1,0:T(4,128)} %copy-done.1, s32[2,4]{1,0:T(2,128)} %copy-done.2, ...), custom_call_target="tpu_custom_call" | custom-call | flops 14000000000 | bytes 1048576 | tf_op jit(solution)/shard_map/previous_gradients/pallas_call | solution.py:99
  62.4 0.1 collective-permute-start.9
  62.5 1.9 %collective-permute-start.12 = (bf16[4,2,2,128,128]{4,3,2,1,0:T(8,128)(2,1)S(1)}, bf16[4,2,2,128,128]{4,3,2,1,0:T(8,128)(2,1)S(1)}, u32[]{:S(2)}, u32[]{:S(2)}) collective-permute-start(bf16[4,2,2,128,128]{4,3,2,1,0:T(8,128)(2,1)S(1)} %get-tuple-element.83), channel_id=1, source_target_pairs={{8,0},{16,8},{24,16},{9,1},{17,9},{25,17},{10,2},{18,10},{26,18},{... | collective-permute-start | bytes 1572872 | tf_op jit(solution)/shard_map/ppermute | solution.py:509
  64.4 1.0 far_current_gradients.1
  65.4 3.0 %collective-permute-done.9 = bf16[2,2,2,128,128]{4,3,2,1,0:T(8,128)(2,1)S(1)} collective-permute-done((bf16[2,2,2,128,128]{4,3,2,1,0:T(8,128)(2,1)S(1)}, bf16[2,2,2,128,128]{4,3,2,1,0:T(8,128)(2,1)S(1)}, u32[]{:S(2)}, u32[]{:S(2)}) %collective-permute-start.9) | collective-permute-done | bytes 262176 | tf_op jit(solution)/shard_map/ppermute | solution.py:500
  68.4 0.1 add_convert_fusion.2
  68.5 0.0 copy-start
  68.5 2.1 %collective-permute-start.10 = (bf16[2,2,2,128,128]{4,3,2,1,0:T(8,128)(2,1)S(1)}, bf16[2,2,2,128,128]{4,3,2,1,0:T(8,128)(2,1)S(1)}, u32[]{:S(2)}, u32[]{:S(2)}) collective-permute-start(bf16[2,2,2,128,128]{4,3,2,1,0:T(8,128)(2,1)S(1)} %add_convert_fusion.2), channel_id=1, source_target_pairs={{8,0},{16,8},{24,16},{9,1},{17,9},{25,17},{10,2},{18,10},{26,18},{... | collective-permute-start | bytes 786440 | tf_op jit(solution)/shard_map/ppermute | solution.py:509
  70.5 0.4 collective-permute-start.11
  70.9 4.3 %near_current_gradients.1 = (f32[2,2,2,128,128]{4,3,2,1,0:T(8,128)S(1)}, f32[2,2,2,128,128]{4,3,2,1,0:T(8,128)S(1)}, bf16[2,4,2,2,128,1024]{5,4,3,2,1,0:T(8,128)(2,1)}) custom-call(s32[2,4,13]{2,1,0:T(4,128)} %copy-done.1, s32[2,4]{1,0:T(2,128)} %copy-done.2, bf16[2,2,8,128,128]{4,3,2,1,0:T(8,128)(2,1)S(1)} %get-tuple-element.59.own, ...), custom_call_target="tpu_custom_call" | custom-call | flops 6000000000 | bytes 1048576 | tf_op jit(solution)/shard_map/near_current_gradients/pallas_call | solution.py:99
  75.1 6.4 %collective-permute-done.10 = bf16[2,2,2,128,128]{4,3,2,1,0:T(8,128)(2,1)S(1)} collective-permute-done((bf16[2,2,2,128,128]{4,3,2,1,0:T(8,128)(2,1)S(1)}, bf16[2,2,2,128,128]{4,3,2,1,0:T(8,128)(2,1)S(1)}, u32[]{:S(2)}, u32[]{:S(2)}) %collective-permute-start.10) | collective-permute-done | bytes 262176 | tf_op jit(solution)/shard_map/ppermute | solution.py:509
  81.5 0.0 collective-permute-done.11
  81.5 0.1 add_convert_fusion.1
  81.6 0.1 collective-permute-start.16
  81.7 0.0 collective-permute-done.12
  81.7 0.1 add_convert_fusion
  81.8 1.2 %collective-permute-start.15 = (bf16[2,2,2,128,128]{4,3,2,1,0:T(8,128)(2,1)S(1)}, bf16[2,2,2,128,128]{4,3,2,1,0:T(8,128)(2,1)S(1)}, u32[]{:S(2)}, u32[]{:S(2)}) collective-permute-start(bf16[2,2,2,128,128]{4,3,2,1,0:T(8,128)(2,1)S(1)} %add_convert_fusion), channel_id=1, source_target_pairs={{0,2},{1,3},{2,0},{3,1},{4,6},{5,7},{6,4},{7,5},{8,10},{9,11},{10,... | collective-permute-start | bytes 786440 | tf_op jit(solution)/shard_map/ppermute | solution.py:500
  83.0 0.0 copy-done
  83.0 10.1 %query_results.1 = (bf16[2,128,1024]{2,1,0:T(8,128)(2,1)S(1)}, bf16[2,128,1024]{2,1,0:T(8,128)(2,1)S(1)}, bf16[2,128,1024]{2,1,0:T(8,128)(2,1)S(1)}, bf16[2,128,1024]{2,1,0:T(8,128)(2,1)S(1)}) custom-call(s32[2,4,13]{2,1,0:T(4,128)} %copy-done.1, s32[2,4]{1,0:T(2,128)} %copy-done.2, s32[32]{0:T(128)} %place_ref.6, ...), custom_call_target="tpu_custom_call" | custom-call | flops 20000000000 | bytes 1048576 | tf_op jit(solution)/shard_map/query_results/pallas_call | solution.py:99
  93.1 3.4 %collective-permute-start.13 = (bf16[2,128,1024]{2,1,0:T(8,128)(2,1)S(1)}, bf16[2,128,1024]{2,1,0:T(8,128)(2,1)S(1)}, u32[]{:S(2)}, u32[]{:S(2)}) collective-permute-start(bf16[2,128,1024]{2,1,0:T(8,128)(2,1)S(1)} %get-tuple-element.89), channel_id=1, source_target_pairs={{0,1},{1,0},{2,3},{3,2},{4,5},{5,4},{6,7},{7,6},{8,9},{9,8},{10,11... | collective-permute-start | bytes 1572872 | tf_op jit(solution)/shard_map/ppermute | solution.py:500
  96.5 0.1 collective-permute-start.14
  96.6 0.0 collective-permute-done.16.rest_3_
  96.6 0.0 collective-permute-done.15.rest_2_
  96.6 0.9 key_gradients.1
  97.5 0.5 collective-permute-start.17
  98.0 1.0 collective-permute-done.17.refs_5_
  99.0 0.0 collective-permute-done.13.refs_2_
  99.0 0.0 collective-permute-done.14.refs_3_
  99.0 1.6 %join_halves.1 = (bf16[128,4096]{1,0:T(8,128)(2,1)}, bf16[128,4096]{1,0:T(8,128)(2,1)}, bf16[128,512]{1,0:T(8,128)(2,1)}, bf16[128,512]{1,0:T(8,128)(2,1)}) custom-call(bf16[2,128,1024]{2,1,0:T(8,128)(2,1)S(1)} %get-tuple-element.80.refs_0_, bf16[2,128,1024]{2,1,0:T(8,128)(2,1)S(1)} %get-tuple-element.86.refs_1_, ...), custom_call_target="tpu_custom_call" | custom-call | flops 2000000000 | bytes 1048576 | tf_op jit(solution)/shard_map/join_halves/pallas_call | solution.py:99
  (2 shorter events, 0.0 us)
Async XLA Ops:
  2.5 2.1 %collective-permute-start = (bf16[2,2,128,128]{3,2,1,0:T(8,128)(2,1)S(1)}, bf16[2,2,128,128]{3,2,1,0:T(8,128)(2,1)S(1)}, u32[]{:S(2)}, u32[]{:S(2)}) collective-permute-start(bf16[2,2,128,128]{3,2,1,0:T(8,128)(2,1)S(1)} %get-tuple-element.51), channel_id=1, source_target_pairs={{0,1},{1,0},{2,3},{3,2},{4,5},{5,4},{6,7},{7,6},{8,9},{9,8},{10,11... | collective-permute-start | bytes 393224 | tf_op jit(solution)/shard_map/ppermute | solution.py:500
  4.7 12.5 %collective-permute-start.3 = (bf16[2,2,2,128,128]{4,3,2,1,0:T(8,128)(2,1)S(1)}, bf16[2,2,2,128,128]{4,3,2,1,0:T(8,128)(2,1)S(1)}, u32[]{:S(2)}, u32[]{:S(2)}) collective-permute-start(bf16[2,2,2,128,128]{4,3,2,1,0:T(8,128)(2,1)S(1)} %pad_maximum_fusion.rest_0_.rest_7_), channel_id=1, source_target_pairs={{0,8},{8,16},{16,24},{1,9},{9,17},{17,25},{2,10},{10,18},{18,26},{... | collective-permute-start | bytes 786440 | tf_op jit(solution)/shard_map/ppermute | solution.py:506
  7.8 13.2 %collective-permute-start.2 = (bf16[2,2,2,128,128]{4,3,2,1,0:T(8,128)(2,1)S(1)}, bf16[2,2,2,128,128]{4,3,2,1,0:T(8,128)(2,1)S(1)}, u32[]{:S(2)}, u32[]{:S(2)}) collective-permute-start(bf16[2,2,2,128,128]{4,3,2,1,0:T(8,128)(2,1)S(1)} %pad_maximum_fusion.rest_0_.rest_7_), channel_id=1, source_target_pairs={{0,2},{1,3},{2,0},{3,1},{4,6},{5,7},{6,4},{7,5},{8,10},{9,11},{10,... | collective-permute-start | bytes 786440 | tf_op jit(solution)/shard_map/ppermute | solution.py:500
  9.1 11.8 %collective-permute-start.1 = (bf16[2,2,2,128,128]{4,3,2,1,0:T(8,128)(2,1)S(1)}, bf16[2,2,2,128,128]{4,3,2,1,0:T(8,128)(2,1)S(1)}, u32[]{:S(2)}, u32[]{:S(2)}) collective-permute-start(bf16[2,2,2,128,128]{4,3,2,1,0:T(8,128)(2,1)S(1)} %pad_maximum_fusion.rest_0_.rest_7_), channel_id=1, source_target_pairs={{0,4},{1,5},{2,6},{3,7},{4,0},{5,1},{6,2},{7,3},{8,12},{9,13},{10,... | collective-permute-start | bytes 786440 | tf_op jit(solution)/shard_map/ppermute | solution.py:500
  13.5 0.6 copy-start.1
  14.1 12.6 %copy-start.2 = (s32[2,4]{1,0:T(2,128)}, s32[2,4]{1,0:T(2,128)S(1)}, u32[]{:S(2)}) copy-start(s32[2,4]{1,0:T(2,128)S(1)} %get-tuple-element.58.counts) | copy-start | bytes 100
  21.0 5.8 %collective-permute-start.4 = (bf16[2,2,8,128,128]{4,3,2,1,0:T(8,128)(2,1)S(1)}, bf16[2,2,8,128,128]{4,3,2,1,0:T(8,128)(2,1)S(1)}, u32[]{:S(2)}, u32[]{:S(2)}) collective-permute-start(bf16[2,2,8,128,128]{4,3,2,1,0:T(8,128)(2,1)S(1)} %get-tuple-element.60), channel_id=1, source_target_pairs={{0,1},{1,0},{2,3},{3,2},{4,5},{5,4},{6,7},{7,6},{8,9},{9,8},{10,11... | collective-permute-start | bytes 3145736 | tf_op jit(solution)/shard_map/ppermute | solution.py:500
  24.4 13.9 %collective-permute-start.6 = (bf16[2,2,2,128,128]{4,3,2,1,0:T(8,128)(2,1)S(1)}, bf16[2,2,2,128,128]{4,3,2,1,0:T(8,128)(2,1)S(1)}, u32[]{:S(2)}, u32[]{:S(2)}) collective-permute-start(bf16[2,2,2,128,128]{4,3,2,1,0:T(8,128)(2,1)S(1)} %collective-permute-done.1.rest_1_.rest_0_.rest_9_), channel_id=1, source_target_pairs={{0,2},{1,3},{2,0},{3,1},{4,6},{5,7},{6,4},{7,5},{8,10},{9,11},{10,... | collective-permute-start | bytes 786440 | tf_op jit(solution)/shard_map/ppermute | solution.py:500
  24.6 10.4 %collective-permute-start.5 = (bf16[2,2,2,128,128]{4,3,2,1,0:T(8,128)(2,1)S(1)}, bf16[2,2,2,128,128]{4,3,2,1,0:T(8,128)(2,1)S(1)}, u32[]{:S(2)}, u32[]{:S(2)}) collective-permute-start(bf16[2,2,2,128,128]{4,3,2,1,0:T(8,128)(2,1)S(1)} %collective-permute-done.1.rest_1_.rest_0_.rest_9_), channel_id=1, source_target_pairs={{0,8},{8,16},{16,24},{1,9},{9,17},{17,25},{2,10},{10,18},{18,26},{... | collective-permute-start | bytes 786440 | tf_op jit(solution)/shard_map/ppermute | solution.py:506
  35.0 9.5 %collective-permute-start.7 = (bf16[2,2,2,128,128]{4,3,2,1,0:T(8,128)(2,1)S(1)}, bf16[2,2,2,128,128]{4,3,2,1,0:T(8,128)(2,1)S(1)}, u32[]{:S(2)}, u32[]{:S(2)}) collective-permute-start(bf16[2,2,2,128,128]{4,3,2,1,0:T(8,128)(2,1)S(1)} %collective-permute-done.2.rest_1_.rest_8_), channel_id=1, source_target_pairs={{0,8},{8,16},{16,24},{1,9},{9,17},{17,25},{2,10},{10,18},{18,26},{... | collective-permute-start | bytes 786440 | tf_op jit(solution)/shard_map/ppermute | solution.py:506
  36.9 7.6 %collective-permute-start.8 = (bf16[2,2,2,128,128]{4,3,2,1,0:T(8,128)(2,1)S(1)}, bf16[2,2,2,128,128]{4,3,2,1,0:T(8,128)(2,1)S(1)}, u32[]{:S(2)}, u32[]{:S(2)}) collective-permute-start(bf16[2,2,2,128,128]{4,3,2,1,0:T(8,128)(2,1)S(1)} %collective-permute-done.5.rest_2_.rest_5_), channel_id=1, source_target_pairs={{0,2},{1,3},{2,0},{3,1},{4,6},{5,7},{6,4},{7,5},{8,10},{9,11},{10,... | collective-permute-start | bytes 786440 | tf_op jit(solution)/shard_map/ppermute | solution.py:500
  62.4 6.0 %collective-permute-start.9 = (bf16[2,2,2,128,128]{4,3,2,1,0:T(8,128)(2,1)S(1)}, bf16[2,2,2,128,128]{4,3,2,1,0:T(8,128)(2,1)S(1)}, u32[]{:S(2)}, u32[]{:S(2)}) collective-permute-start(bf16[2,2,2,128,128]{4,3,2,1,0:T(8,128)(2,1)S(1)} %get-tuple-element.66), channel_id=1, source_target_pairs={{0,2},{1,3},{2,0},{3,1},{4,6},{5,7},{6,4},{7,5},{8,10},{9,11},{10,... | collective-permute-start | bytes 786440 | tf_op jit(solution)/shard_map/ppermute | solution.py:500
  62.5 19.2 %collective-permute-start.12 = (bf16[4,2,2,128,128]{4,3,2,1,0:T(8,128)(2,1)S(1)}, bf16[4,2,2,128,128]{4,3,2,1,0:T(8,128)(2,1)S(1)}, u32[]{:S(2)}, u32[]{:S(2)}) collective-permute-start(bf16[4,2,2,128,128]{4,3,2,1,0:T(8,128)(2,1)S(1)} %get-tuple-element.83), channel_id=1, source_target_pairs={{8,0},{16,8},{24,16},{9,1},{17,9},{25,17},{10,2},{18,10},{26,18},{... | collective-permute-start | bytes 1572872 | tf_op jit(solution)/shard_map/ppermute | solution.py:509
  68.5 14.5 %copy-start = (f32[320,128]{1,0:T(8,128)S(1)}, f32[320,128]{1,0:T(8,128)}, u32[]{:S(2)}) copy-start(f32[320,128]{1,0:T(8,128)} %constant.2.clone.refs_2_.rest_11_.rest_4_) | copy-start | bytes 491524
  68.5 13.1 %collective-permute-start.10 = (bf16[2,2,2,128,128]{4,3,2,1,0:T(8,128)(2,1)S(1)}, bf16[2,2,2,128,128]{4,3,2,1,0:T(8,128)(2,1)S(1)}, u32[]{:S(2)}, u32[]{:S(2)}) collective-permute-start(bf16[2,2,2,128,128]{4,3,2,1,0:T(8,128)(2,1)S(1)} %add_convert_fusion.2), channel_id=1, source_target_pairs={{8,0},{16,8},{24,16},{9,1},{17,9},{25,17},{10,2},{18,10},{26,18},{... | collective-permute-start | bytes 786440 | tf_op jit(solution)/shard_map/ppermute | solution.py:509
  70.5 11.0 %collective-permute-start.11 = (bf16[2,2,2,128,128]{4,3,2,1,0:T(8,128)(2,1)S(1)}, bf16[2,2,2,128,128]{4,3,2,1,0:T(8,128)(2,1)S(1)}, u32[]{:S(2)}, u32[]{:S(2)}) collective-permute-start(bf16[2,2,2,128,128]{4,3,2,1,0:T(8,128)(2,1)S(1)} %get-tuple-element.74), channel_id=1, source_target_pairs={{0,2},{1,3},{2,0},{3,1},{4,6},{5,7},{6,4},{7,5},{8,10},{9,11},{10,... | collective-permute-start | bytes 786440 | tf_op jit(solution)/shard_map/ppermute | solution.py:500
  81.6 15.0 %collective-permute-start.16 = (bf16[2,2,2,128,128]{4,3,2,1,0:T(8,128)(2,1)S(1)}, bf16[2,2,2,128,128]{4,3,2,1,0:T(8,128)(2,1)S(1)}, u32[]{:S(2)}, u32[]{:S(2)}) collective-permute-start(bf16[2,2,2,128,128]{4,3,2,1,0:T(8,128)(2,1)S(1)} %add_convert_fusion.1), channel_id=1, source_target_pairs={{0,4},{1,5},{2,6},{3,7},{4,0},{5,1},{6,2},{7,3},{8,12},{9,13},{10,... | collective-permute-start | bytes 786440 | tf_op jit(solution)/shard_map/ppermute | solution.py:500
  81.8 14.9 %collective-permute-start.15 = (bf16[2,2,2,128,128]{4,3,2,1,0:T(8,128)(2,1)S(1)}, bf16[2,2,2,128,128]{4,3,2,1,0:T(8,128)(2,1)S(1)}, u32[]{:S(2)}, u32[]{:S(2)}) collective-permute-start(bf16[2,2,2,128,128]{4,3,2,1,0:T(8,128)(2,1)S(1)} %add_convert_fusion), channel_id=1, source_target_pairs={{0,2},{1,3},{2,0},{3,1},{4,6},{5,7},{6,4},{7,5},{8,10},{9,11},{10,... | collective-permute-start | bytes 786440 | tf_op jit(solution)/shard_map/ppermute | solution.py:500
  93.1 5.9 %collective-permute-start.13 = (bf16[2,128,1024]{2,1,0:T(8,128)(2,1)S(1)}, bf16[2,128,1024]{2,1,0:T(8,128)(2,1)S(1)}, u32[]{:S(2)}, u32[]{:S(2)}) collective-permute-start(bf16[2,128,1024]{2,1,0:T(8,128)(2,1)S(1)} %get-tuple-element.89), channel_id=1, source_target_pairs={{0,1},{1,0},{2,3},{3,2},{4,5},{5,4},{6,7},{7,6},{8,9},{9,8},{10,11... | collective-permute-start | bytes 1572872 | tf_op jit(solution)/shard_map/ppermute | solution.py:500
  96.5 2.5 %collective-permute-start.14 = (bf16[2,128,1024]{2,1,0:T(8,128)(2,1)S(1)}, bf16[2,128,1024]{2,1,0:T(8,128)(2,1)S(1)}, u32[]{:S(2)}, u32[]{:S(2)}) collective-permute-start(bf16[2,128,1024]{2,1,0:T(8,128)(2,1)S(1)} %get-tuple-element.90), channel_id=1, source_target_pairs={{0,1},{1,0},{2,3},{3,2},{4,5},{5,4},{6,7},{7,6},{8,9},{9,8},{10,11... | collective-permute-start | bytes 1572872 | tf_op jit(solution)/shard_map/ppermute | solution.py:500
  97.5 1.5 %collective-permute-start.17 = (bf16[2,128,256]{2,1,0:T(8,128)(2,1)S(1)}, bf16[2,128,256]{2,1,0:T(8,128)(2,1)S(1)}, u32[]{:S(2)}, u32[]{:S(2)}) collective-permute-start(bf16[2,128,256]{2,1,0:T(8,128)(2,1)S(1)} %get-tuple-element.95), channel_id=1, source_target_pairs={{0,1},{1,0},{2,3},{3,2},{4,5},{5,4},{6,7},{7,6},{8,9},{9,8},{10,11... | collective-permute-start | bytes 393224 | tf_op jit(solution)/shard_map/ppermute | solution.py:500

commit v3 on v0

--- a/solution.py
+++ b/solution.py
@@ -73,11 +73,11 @@
     return math.prod(array.shape) * jnp.dtype(array.dtype).itemsize
 
 
-def call(kernel, out_shape, n_smem, scratch=(), us=1, name=None, n_hbm=0, hbm_out=None, pin=False):
+def call(kernel, out_shape, n_smem, scratch=(), us=1, name=None, n_hbm=0, hbm_out=None, hold=()):
     def placed(n, a):
         if n == hbm_out:
             return pltpu.HBM(a.shape, a.dtype)
-        return pltpu.VMEM(a.shape, a.dtype) if pin else a
+        return a
 
     def spec(n, a):
         if a.dtype == jnp.int32:
@@ -93,7 +93,7 @@
         in_specs = [SMEM_SPEC] * n_smem + [HBM_SPEC] * n_hbm
         in_specs += [VMEM_SPEC] * (len(arrays) - n_left)
         pinned = [
-            pltpu.with_memory_space_constraint(a, pltpu.HBM) if n < n_left else a
+            pltpu.with_memory_space_constraint(a, pltpu.HBM) if n < n_left or n in hold else a
             for n, a in enumerate(arrays)
         ]
         results = pl.pallas_call(
@@ -113,41 +113,51 @@
     return run
 
 
-def fetch(sources, places, sems):
-    copies = [
-        pltpu.make_async_copy(source, place, sems.at[n])
-        for n, (source, place) in enumerate(zip(sources, places))
-    ]
-    for copy in copies:
+def prepare(n_seq, place_ref, *refs):
+    key, value, query, grad, table_hbm, kv_keep, kv_send, q_keep, q_send = refs[:9]
+    key_here, table, query_here, kept, sems = refs[9:]
+    group, member, core = here(n_seq)
+    width = HEADS // CORES * HEAD_DIM
+    started = []
+
+    def start(source, place):
+        copy = pltpu.make_async_copy(source, place, sems.at[len(started)])
         copy.start()
-    for copy in copies:
+        started.append(copy)
+        return copy
+
+    def columns(first, count=1):
+        return pl.ds(pl.multiple_of(first * HEAD_DIM, HEAD_DIM), count * HEAD_DIM)
+
+    waits = [start(key, key_here), start(table_hbm, table)]
+    halves = (1 - core, core)
+    loads = []
+    for n, half in enumerate(halves):
+        loads.append(start(query.at[:, columns(half * (HEADS // CORES), HEADS // CORES)], query_here.at[n]))
+    late = []
+    for half, kv_out, q_out in ((halves[0], kv_send, q_send), (halves[1], kv_keep, q_keep)):
+        for h in range(HALF_KV):
+            head = half * HALF_KV + h
+            late.append(start(value.at[:, columns(head)], kv_out.at[1, h]))
+            for r in range(RATIO):
+                late.append(start(grad.at[:, columns(head * RATIO + r)], q_out.at[1, h, r]))
+    for copy in waits:
         copy.wait()
-
-
-def prepare_kv(n_seq, place_ref, *refs):
-    sources, (keep, send), (key, value, table, sems) = refs[:3], refs[3:5], refs[5:]
-    fetch(sources, (key, value, table), sems)
-    group, member, core = here(n_seq)
     cosine, sine = block_tables(place_ref[group * n_seq + member], table)
-    for out, half in ((keep, core), (send, 1 - core)):
+    for half, out in ((halves[0], kv_send), (halves[1], kv_keep)):
         for h in range(HALF_KV):
-            columns = pl.ds(pl.multiple_of((half * HALF_KV + h) * HEAD_DIM, HEAD_DIM), HEAD_DIM)
-            out[0, h] = turn(key[:, columns].astype(F32), cosine, sine).astype(BF16)
-            out[1, h] = value[:, columns]
-
-
-def prepare_queries(n_seq, place_ref, *refs):
-    sources, (keep, send), (query, grad, table, sems) = refs[:3], refs[3:5], refs[5:]
-    fetch(sources, (query, grad, table), sems)
-    group, member, core = here(n_seq)
-    cosine, sine = block_tables(place_ref[group * n_seq + member], table)
-    for out, half in ((keep, core), (send, 1 - core)):
+            part = key_here[:, columns(half * HALF_KV + h)]
+            out[0, h] = turn(part.astype(F32), cosine, sine).astype(BF16)
+    for n, out in enumerate((q_send.at[0], kept)):
+        loads[n].wait()
         for h in range(HALF_KV):
             for r in range(RATIO):
-                head = (half * HALF_KV + h) * RATIO + r
-                columns = pl.ds(pl.multiple_of(head * HEAD_DIM, HEAD_DIM), HEAD_DIM)
-                out[0, h, r] = turn(query[:, columns].astype(F32), cosine, sine).astype(BF16)
-                out[1, h, r] = grad[:, columns]
+                at = (h * RATIO + r) * HEAD_DIM
+                part = query_here[n, :, at : at + HEAD_DIM].astype(F32)
+                out[h, r] = turn(part, cosine, sine).astype(BF16)
+    late.append(start(kept, q_keep.at[0]))
+    for copy in late:
+        copy.wait()
 
 
 def make_lists(n_seq, split, key_blocks, key_counts, lists, counts):
@@ -528,30 +538,33 @@
         2, us=2, name="block_lists",
     )(key_blocks, key_counts)
 
-    def prepared(kernel, shape, first, second, name):
-        held = [pltpu.VMEM(a.shape, a.dtype) for a in (first, second, table)]
-        return call(
-            functools.partial(kernel, n_seq), (shape, shape), 1,
-            [*held, pltpu.SemaphoreType.DMA((3,))], us=1, name=name, n_hbm=3, pin=True,
-        )(block_position, first, second, table)
-
-    kv_keep, kv_send = prepared(prepare_kv, kv_shape, key_input, value_input, "rotate_keys")
+    tokens = query_input.shape[0]
+    n_copies = 5 + 2 * HALF_KV * (1 + RATIO)
+    kv_keep, kv_send, q_keep, q_send = call(
+        functools.partial(prepare, n_seq), (kv_shape, kv_shape, q_shape, q_shape), 1,
+        [
+            pltpu.VMEM(key_input.shape, BF16), pltpu.VMEM(table.shape, F32),
+            pltpu.VMEM((CORES, tokens, HEADS // CORES * HEAD_DIM), BF16),
+            pltpu.VMEM(q_shape.shape[1:], BF16), pltpu.SemaphoreType.DMA((n_copies,)),
+        ],
+        us=3, name="prepare", n_hbm=5, hbm_out=2,
+    )(block_position, key_input, value_input, query_input, out_grad, table)
     kv_got = cross(kv_send, 1)
-    query_late, kv_keep = lax.optimization_barrier((query_input, kv_keep))
-    q_keep, q_send = prepared(prepare_queries, q_shape, query_late, out_grad, "rotate_queries")
-    q_send, q_keep, kv_got, kv_keep = lax.optimization_barrier((q_send, q_keep, kv_got, kv_keep))
+    q_send, kv_got = lax.optimization_barrier((q_send, kv_got))
     q_got = cross(q_send, 1)
     near = [jnp.stack([kv_keep, kv_got])]
     near.append(along(near[0], 1))
     ready, first_far = lax.optimization_barrier((near[1], onward(near[0])))
     far = [first_far, None]
     for k in range(2, n_pieces, 2):
-        piece_k, _ = lax.optimization_barrier((along(near[0], k), ready))
+        piece_k, lists, counts, _ = lax.optimization_barrier(
+            (along(near[0], k), lists, counts, ready)
+        )
         near += [piece_k, along(piece_k, 1)]
         far += [onward(piece_k), None]
     stats = call(
         functools.partial(current_stats, 1), stats_shape, 2, [pltpu.VMEM((split, *piece), BF16)],
-        us=4, name="near_statistics",
+        us=4, name="near_statistics", hold=(2,),
     )(lists, counts, q_keep, q_got, *near[:2])
     ready, far[2], stats = lax.optimization_barrier((ready, far[2], stats))
     far[1] = onward(ready)

time: 102 us -> 114 us (1.12)
  the two profiles are of different devices: /device:TPU:5 before, /device:TPU:3 now
where the time goes in v3:
time: 114 us; the launch traced here: 116 us
  Pallas kernels  61.1 us (54%)
  starting transfers between devices  28.7 us (25%)
  waiting for transfers between devices  23.4 us (21%)
  local copies, waits for them, and re-layouts  1.31 us (1%)
    pallas_call x10, Pallas kernels, run(): pl.pallas_call(kernel, out_shape=[placed(n, a) for n, a in enumerate(outs...  61.1 us
    ppermute x13, starting transfers between devices, cross(): return lax.ppermute(array, 'seq', [(m, m ^ by) for m in range(n_seq)])  14.5 us
    ppermute x13, waiting for transfers between devices, cross(): return lax.ppermute(array, 'seq', [(m, m ^ by) for m in range(n_seq)])  12.5 us
    ppermute x3, starting transfers between devices, onward(): return lax.ppermute(array, 'grp', [(g, g + 1) for g in range(n_grp - 1)])  10.2 us
    ppermute x2, waiting for transfers between devices, back(): return lax.ppermute(array, 'grp', [(g + 1, g) for g in range(n_grp - 1)])  6.45 us
    ppermute x3, waiting for transfers between devices, onward(): return lax.ppermute(array, 'grp', [(g, g + 1) for g in range(n_grp - 1)])  4.42 us
    ppermute x2, starting transfers between devices, back(): return lax.ppermute(array, 'grp', [(g + 1, g) for g in range(n_grp - 1)])  3.97 us
  transfers between devices with their start and end apart: 18, of which 8 were waited for; matrix products, arithmetic and copies ran while one was open for 1% of the time, Pallas kernels for 20%

profile of v3, /device:TPU:3, one launch (start us, length us, event | category | flops | bytes accessed | tf_op | source)
XLA Modules:
  0.0 115.7 jit_solution(6919919077727640213)
XLA Ops:
  0.6 0.0 copy-start.4
  0.6 18.2 %prepare.1 = (bf16[2,2,128,128]{3,2,1,0:T(8,128)(2,1)S(1)}, bf16[2,2,128,128]{3,2,1,0:T(8,128)(2,1)S(1)}, bf16[2,2,8,128,128]{4,3,2,1,0:T(8,128)(2,1)}, bf16[2,2,8,128,128]{4,3,2,1,0:T(8,128)(2,1)S(1)}) custom-call(s32[32]{0:T(128)} %place_ref.4, bf16[128,512]{1,0:T(8,128)(2,1)} %refs_0_.1, bf16[128,512]{1,0:T(8,128)(2,1)} %refs_1_.1, ...), custom_call_target="tpu_custom_call" | custom-call | flops 3000000000 | bytes 1048576 | tf_op jit(solution)/shard_map/prepare/pallas_call | solution.py:99
  18.9 0.7 collective-permute-start
  19.6 1.0 collective-permute-done
  20.6 0.4 collective-permute-start.4
  21.0 3.1 %collective-permute-start.3 = (bf16[2,2,2,128,128]{4,3,2,1,0:T(8,128)(2,1)S(1)}, bf16[2,2,2,128,128]{4,3,2,1,0:T(8,128)(2,1)S(1)}, u32[]{:S(2)}, u32[]{:S(2)}) collective-permute-start(bf16[2,2,2,128,128]{4,3,2,1,0:T(8,128)(2,1)S(1)} %pad_maximum_fusion.rest_0_.rest_7_), channel_id=1, source_target_pairs={{0,8},{8,16},{16,24},{1,9},{9,17},{17,25},{2,10},{10,18},{18,26},{... | collective-permute-start | bytes 786440 | tf_op jit(solution)/shard_map/ppermute | solution.py:517
  24.1 1.4 %collective-permute-start.2 = (bf16[2,2,2,128,128]{4,3,2,1,0:T(8,128)(2,1)S(1)}, bf16[2,2,2,128,128]{4,3,2,1,0:T(8,128)(2,1)S(1)}, u32[]{:S(2)}, u32[]{:S(2)}) collective-permute-start(bf16[2,2,2,128,128]{4,3,2,1,0:T(8,128)(2,1)S(1)} %pad_maximum_fusion.rest_0_.rest_7_), channel_id=1, source_target_pairs={{0,2},{1,3},{2,0},{3,1},{4,6},{5,7},{6,4},{7,5},{8,10},{9,11},{10,... | collective-permute-start | bytes 786440 | tf_op jit(solution)/shard_map/ppermute | solution.py:511
  25.5 2.3 %collective-permute-start.1 = (bf16[2,2,2,128,128]{4,3,2,1,0:T(8,128)(2,1)S(1)}, bf16[2,2,2,128,128]{4,3,2,1,0:T(8,128)(2,1)S(1)}, u32[]{:S(2)}, u32[]{:S(2)}) collective-permute-start(bf16[2,2,2,128,128]{4,3,2,1,0:T(8,128)(2,1)S(1)} %pad_maximum_fusion.rest_0_.rest_7_), channel_id=1, source_target_pairs={{0,4},{1,5},{2,6},{3,7},{4,0},{5,1},{6,2},{7,3},{8,12},{9,13},{10,... | collective-permute-start | bytes 786440 | tf_op jit(solution)/shard_map/ppermute | solution.py:511
  27.8 0.0 copy-done.4
  27.8 0.7 copy.12.key_blocks
  28.5 2.1 %block_lists.1 = (s32[2,4,13]{2,1,0:T(4,128)S(1)}, s32[2,4]{1,0:T(2,128)S(1)}) custom-call(s32[32,12]{1,0:T(8,128)} %copy.12.key_blocks, s32[32]{0:T(128)} %key_counts.1), custom_call_target="tpu_custom_call" | custom-call | flops 2000000000 | bytes 1048576 | tf_op jit(solution)/shard_map/block_lists/pallas_call | solution.py:99
  30.6 0.0 copy-start.2
  30.6 0.6 copy-done.2
  31.2 0.0 copy-start.3
  31.2 0.0 copy-start.1
  31.2 0.0 collective-permute-done.3.rest_0_.rest_3_
  31.2 5.9 %collective-permute-done.2.rest_1_.rest_8_ = bf16[2,2,2,128,128]{4,3,2,1,0:T(8,128)(2,1)S(1)} collective-permute-done((bf16[2,2,2,128,128]{4,3,2,1,0:T(8,128)(2,1)S(1)}, bf16[2,2,2,128,128]{4,3,2,1,0:T(8,128)(2,1)S(1)}, u32[]{:S(2)}, u32[]{:S(2)}) %collective-permute-start.2) | collective-permute-done | bytes 262176 | tf_op jit(solution)/shard_map/ppermute | solution.py:511
  37.1 0.0 collective-permute-done.1.rest_1_.rest_0_.rest_9_
  37.1 2.5 %collective-permute-start.6 = (bf16[2,2,2,128,128]{4,3,2,1,0:T(8,128)(2,1)S(1)}, bf16[2,2,2,128,128]{4,3,2,1,0:T(8,128)(2,1)S(1)}, u32[]{:S(2)}, u32[]{:S(2)}) collective-permute-start(bf16[2,2,2,128,128]{4,3,2,1,0:T(8,128)(2,1)S(1)} %collective-permute-done.1.rest_1_.rest_0_.rest_9_), channel_id=1, source_target_pairs={{0,2},{1,3},{2,0},{3,1},{4,6},{5,7},{6,4},{7,5},{8,10},{9,11},{10,... | collective-permute-start | bytes 786440 | tf_op jit(solution)/shard_map/ppermute | solution.py:511
  39.6 3.1 %collective-permute-start.5 = (bf16[2,2,2,128,128]{4,3,2,1,0:T(8,128)(2,1)S(1)}, bf16[2,2,2,128,128]{4,3,2,1,0:T(8,128)(2,1)S(1)}, u32[]{:S(2)}, u32[]{:S(2)}) collective-permute-start(bf16[2,2,2,128,128]{4,3,2,1,0:T(8,128)(2,1)S(1)} %collective-permute-done.1.rest_1_.rest_0_.rest_9_), channel_id=1, source_target_pairs={{0,8},{8,16},{16,24},{1,9},{9,17},{17,25},{2,10},{10,18},{18,26},{... | collective-permute-start | bytes 786440 | tf_op jit(solution)/shard_map/ppermute | solution.py:517
  42.7 0.0 collective-permute-done.4.other
  42.7 0.0 copy-done.3
  42.7 2.9 %near_statistics.1.rest_0_ = f32[2,2,8,1024]{3,2,1,0:T(8,128)S(1)} custom-call(s32[2,4,13]{2,1,0:T(4,128)} %copy-done.2, s32[2,4]{1,0:T(2,128)} %copy-done.3, bf16[2,2,8,128,128]{4,3,2,1,0:T(8,128)(2,1)} %get-tuple-element.59.own, bf16[2,2,8,128,128]{4,3,2,1,0:T(8,128)(2,1)S(1)} %collective-permute-done.4.other, ...), custom_call_target="tpu_custom_call" | custom-call | flops 4000000000 | bytes 1048576 | tf_op jit(solution)/shard_map/near_statistics/pallas_call | solution.py:99
  45.6 2.0 %collective-permute-done.5.rest_2_.rest_5_ = bf16[2,2,2,128,128]{4,3,2,1,0:T(8,128)(2,1)S(1)} collective-permute-done((bf16[2,2,2,128,128]{4,3,2,1,0:T(8,128)(2,1)S(1)}, bf16[2,2,2,128,128]{4,3,2,1,0:T(8,128)(2,1)S(1)}, u32[]{:S(2)}, u32[]{:S(2)}) %collective-permute-start.5) | collective-permute-done | bytes 262176 | tf_op jit(solution)/shard_map/ppermute | solution.py:517
  47.6 4.0 %collective-permute-start.7 = (bf16[2,2,2,128,128]{4,3,2,1,0:T(8,128)(2,1)S(1)}, bf16[2,2,2,128,128]{4,3,2,1,0:T(8,128)(2,1)S(1)}, u32[]{:S(2)}, u32[]{:S(2)}) collective-permute-start(bf16[2,2,2,128,128]{4,3,2,1,0:T(8,128)(2,1)S(1)} %collective-permute-done.2.rest_1_.rest_8_), channel_id=1, source_target_pairs={{0,8},{8,16},{16,24},{1,9},{9,17},{17,25},{2,10},{10,18},{18,26},{... | collective-permute-start | bytes 786440 | tf_op jit(solution)/shard_map/ppermute | solution.py:517
  51.7 0.1 collective-permute-start.8
  51.7 0.0 collective-permute-done.6.rest_2_.rest_1_.rest_10_
  51.7 0.0 copy-done.1
  51.8 0.8 far_statistics.1.stats_in
  52.6 2.4 %collective-permute-done.7.rest_1_.rest_4_ = bf16[2,2,2,128,128]{4,3,2,1,0:T(8,128)(2,1)S(1)} collective-permute-done((bf16[2,2,2,128,128]{4,3,2,1,0:T(8,128)(2,1)S(1)}, bf16[2,2,2,128,128]{4,3,2,1,0:T(8,128)(2,1)S(1)}, u32[]{:S(2)}, u32[]{:S(2)}) %collective-permute-start.7) | collective-permute-done | bytes 262176 | tf_op jit(solution)/shard_map/ppermute | solution.py:517
  54.9 2.3 %collective-permute-done.8.rest_3_.rest_6_ = bf16[2,2,2,128,128]{4,3,2,1,0:T(8,128)(2,1)S(1)} collective-permute-done((bf16[2,2,2,128,128]{4,3,2,1,0:T(8,128)(2,1)S(1)}, bf16[2,2,2,128,128]{4,3,2,1,0:T(8,128)(2,1)S(1)}, u32[]{:S(2)}, u32[]{:S(2)}) %collective-permute-start.8) | collective-permute-done | bytes 262176 | tf_op jit(solution)/shard_map/ppermute | solution.py:511
  57.2 18.6 %previous_gradients.1 = (bf16[4,2,2,128,128]{4,3,2,1,0:T(8,128)(2,1)S(1)}, bf16[2,2,2,128,128]{4,3,2,1,0:T(8,128)(2,1)S(1)}, bf16[2,2,2,128,128]{4,3,2,1,0:T(8,1...) custom-call(s32[2,4,13]{2,1,0:T(4,128)} %copy-done.2, s32[2,4]{1,0:T(2,128)} %copy-done.3, ...), custom_call_target="tpu_custom_call" | custom-call | flops 14000000000 | bytes 1048576 | tf_op jit(solution)/shard_map/previous_gradients/pallas_call | solution.py:99
  75.8 0.1 collective-permute-start.9
  75.9 1.9 %collective-permute-start.12 = (bf16[4,2,2,128,128]{4,3,2,1,0:T(8,128)(2,1)S(1)}, bf16[4,2,2,128,128]{4,3,2,1,0:T(8,128)(2,1)S(1)}, u32[]{:S(2)}, u32[]{:S(2)}) collective-permute-start(bf16[4,2,2,128,128]{4,3,2,1,0:T(8,128)(2,1)S(1)} %get-tuple-element.83), channel_id=1, source_target_pairs={{8,0},{16,8},{24,16},{9,1},{17,9},{25,17},{10,2},{18,10},{26,18},{... | collective-permute-start | bytes 1572872 | tf_op jit(solution)/shard_map/ppermute | solution.py:520
  77.8 1.0 far_current_gradients.1
  78.8 2.3 %collective-permute-done.9 = bf16[2,2,2,128,128]{4,3,2,1,0:T(8,128)(2,1)S(1)} collective-permute-done((bf16[2,2,2,128,128]{4,3,2,1,0:T(8,128)(2,1)S(1)}, bf16[2,2,2,128,128]{4,3,2,1,0:T(8,128)(2,1)S(1)}, u32[]{:S(2)}, u32[]{:S(2)}) %collective-permute-start.9) | collective-permute-done | bytes 262176 | tf_op jit(solution)/shard_map/ppermute | solution.py:511
  81.1 0.1 add_convert_fusion.2
  81.2 0.0 copy-start
  81.2 2.1 %collective-permute-start.10 = (bf16[2,2,2,128,128]{4,3,2,1,0:T(8,128)(2,1)S(1)}, bf16[2,2,2,128,128]{4,3,2,1,0:T(8,128)(2,1)S(1)}, u32[]{:S(2)}, u32[]{:S(2)}) collective-permute-start(bf16[2,2,2,128,128]{4,3,2,1,0:T(8,128)(2,1)S(1)} %add_convert_fusion.2), channel_id=1, source_target_pairs={{8,0},{16,8},{24,16},{9,1},{17,9},{25,17},{10,2},{18,10},{26,18},{... | collective-permute-start | bytes 786440 | tf_op jit(solution)/shard_map/ppermute | solution.py:520
  83.3 0.1 collective-permute-start.11
  83.3 4.3 %near_current_gradients.1 = (f32[2,2,2,128,128]{4,3,2,1,0:T(8,128)S(1)}, f32[2,2,2,128,128]{4,3,2,1,0:T(8,128)S(1)}, bf16[2,4,2,2,128,1024]{5,4,3,2,1,0:T(8,128)(2,1)}) custom-call(s32[2,4,13]{2,1,0:T(4,128)} %copy-done.2, s32[2,4]{1,0:T(2,128)} %copy-done.3, bf16[2,2,8,128,128]{4,3,2,1,0:T(8,128)(2,1)S(1)} %copy-done.1, ...), custom_call_target="tpu_custom_call" | custom-call | flops 6000000000 | bytes 1048576 | tf_op jit(solution)/shard_map/near_current_gradients/pallas_call | solution.py:99
  87.6 6.4 %collective-permute-done.10 = bf16[2,2,2,128,128]{4,3,2,1,0:T(8,128)(2,1)S(1)} collective-permute-done((bf16[2,2,2,128,128]{4,3,2,1,0:T(8,128)(2,1)S(1)}, bf16[2,2,2,128,128]{4,3,2,1,0:T(8,128)(2,1)S(1)}, u32[]{:S(2)}, u32[]{:S(2)}) %collective-permute-start.10) | collective-permute-done | bytes 262176 | tf_op jit(solution)/shard_map/ppermute | solution.py:520
  94.1 0.0 collective-permute-done.11
  94.1 0.1 add_convert_fusion.1
  94.2 0.1 collective-permute-start.16
  94.2 0.0 collective-permute-done.12
  94.2 0.1 add_convert_fusion
  94.3 1.2 %collective-permute-start.15 = (bf16[2,2,2,128,128]{4,3,2,1,0:T(8,128)(2,1)S(1)}, bf16[2,2,2,128,128]{4,3,2,1,0:T(8,128)(2,1)S(1)}, u32[]{:S(2)}, u32[]{:S(2)}) collective-permute-start(bf16[2,2,2,128,128]{4,3,2,1,0:T(8,128)(2,1)S(1)} %add_convert_fusion), channel_id=1, source_target_pairs={{0,2},{1,3},{2,0},{3,1},{4,6},{5,7},{6,4},{7,5},{8,10},{9,11},{10,... | collective-permute-start | bytes 786440 | tf_op jit(solution)/shard_map/ppermute | solution.py:511
  95.5 0.0 copy-done
  95.5 10.9 %query_results.1 = (bf16[2,128,1024]{2,1,0:T(8,128)(2,1)S(1)}, bf16[2,128,1024]{2,1,0:T(8,128)(2,1)S(1)}, bf16[2,128,1024]{2,1,0:T(8,128)(2,1)S(1)}, bf16[2,128,1024]{2,1,0:T(8,128)(2,1)S(1)}) custom-call(s32[2,4,13]{2,1,0:T(4,128)} %copy-done.2, s32[2,4]{1,0:T(2,128)} %copy-done.3, s32[32]{0:T(128)} %place_ref.4, ...), custom_call_target="tpu_custom_call" | custom-call | flops 20000000000 | bytes 1048576 | tf_op jit(solution)/shard_map/query_results/pallas_call | solution.py:99
  106.4 5.2 %collective-permute-start.13 = (bf16[2,128,1024]{2,1,0:T(8,128)(2,1)S(1)}, bf16[2,128,1024]{2,1,0:T(8,128)(2,1)S(1)}, u32[]{:S(2)}, u32[]{:S(2)}) collective-permute-start(bf16[2,128,1024]{2,1,0:T(8,128)(2,1)S(1)} %get-tuple-element.89), channel_id=1, source_target_pairs={{0,1},{1,0},{2,3},{3,2},{4,5},{5,4},{6,7},{7,6},{8,9},{9,8},{10,11... | collective-permute-start | bytes 1572872 | tf_op jit(solution)/shard_map/ppermute | solution.py:511
  111.6 0.1 collective-permute-start.14
  111.7 0.0 collective-permute-done.16.rest_3_
  111.7 0.0 collective-permute-done.15.rest_2_
  111.7 0.9 key_gradients.1
  112.6 0.5 collective-permute-start.17
  113.1 1.0 collective-permute-done.17.refs_5_
  114.1 0.0 collective-permute-done.13.refs_2_
  114.1 0.0 collective-permute-done.14.refs_3_
  114.1 1.6 %join_halves.1 = (bf16[128,4096]{1,0:T(8,128)(2,1)}, bf16[128,4096]{1,0:T(8,128)(2,1)}, bf16[128,512]{1,0:T(8,128)(2,1)}, bf16[128,512]{1,0:T(8,128)(2,1)}) custom-call(bf16[2,128,1024]{2,1,0:T(8,128)(2,1)S(1)} %get-tuple-element.80.refs_0_, bf16[2,128,1024]{2,1,0:T(8,128)(2,1)S(1)} %get-tuple-element.86.refs_1_, ...), custom_call_target="tpu_custom_call" | custom-call | flops 2000000000 | bytes 1048576 | tf_op jit(solution)/shard_map/join_halves/pallas_call | solution.py:99
  (2 shorter events, 0.0 us)
Async XLA Ops:
  0.6 27.1 %copy-start.4 = (s32[32,12]{0,1:T(8,128)S(1)}, s32[32,12]{0,1:T(8,128)}, u32[]{:S(2)}) copy-start(s32[32,12]{0,1:T(8,128)} %param.12) | copy-start | bytes 4612
  18.9 1.7 %collective-permute-start = (bf16[2,2,128,128]{3,2,1,0:T(8,128)(2,1)S(1)}, bf16[2,2,128,128]{3,2,1,0:T(8,128)(2,1)S(1)}, u32[]{:S(2)}, u32[]{:S(2)}) collective-permute-start(bf16[2,2,128,128]{3,2,1,0:T(8,128)(2,1)S(1)} %get-tuple-element.52), channel_id=1, source_target_pairs={{0,1},{1,0},{2,3},{3,2},{4,5},{5,4},{6,7},{7,6},{8,9},{9,8},{10,11... | collective-permute-start | bytes 393224 | tf_op jit(solution)/shard_map/ppermute | solution.py:511
  20.6 22.1 %collective-permute-start.4 = (bf16[2,2,8,128,128]{4,3,2,1,0:T(8,128)(2,1)S(1)}, bf16[2,2,8,128,128]{4,3,2,1,0:T(8,128)(2,1)S(1)}, u32[]{:S(2)}, u32[]{:S(2)}) collective-permute-start(bf16[2,2,8,128,128]{4,3,2,1,0:T(8,128)(2,1)S(1)} %get-tuple-element.60), channel_id=1, source_target_pairs={{0,1},{1,0},{2,3},{3,2},{4,5},{5,4},{6,7},{7,6},{8,9},{9,8},{10,11... | collective-permute-start | bytes 3145736 | tf_op jit(solution)/shard_map/ppermute | solution.py:511
  21.0 10.2 %collective-permute-start.3 = (bf16[2,2,2,128,128]{4,3,2,1,0:T(8,128)(2,1)S(1)}, bf16[2,2,2,128,128]{4,3,2,1,0:T(8,128)(2,1)S(1)}, u32[]{:S(2)}, u32[]{:S(2)}) collective-permute-start(bf16[2,2,2,128,128]{4,3,2,1,0:T(8,128)(2,1)S(1)} %pad_maximum_fusion.rest_0_.rest_7_), channel_id=1, source_target_pairs={{0,8},{8,16},{16,24},{1,9},{9,17},{17,25},{2,10},{10,18},{18,26},{... | collective-permute-start | bytes 786440 | tf_op jit(solution)/shard_map/ppermute | solution.py:517
  24.1 13.0 %collective-permute-start.2 = (bf16[2,2,2,128,128]{4,3,2,1,0:T(8,128)(2,1)S(1)}, bf16[2,2,2,128,128]{4,3,2,1,0:T(8,128)(2,1)S(1)}, u32[]{:S(2)}, u32[]{:S(2)}) collective-permute-start(bf16[2,2,2,128,128]{4,3,2,1,0:T(8,128)(2,1)S(1)} %pad_maximum_fusion.rest_0_.rest_7_), channel_id=1, source_target_pairs={{0,2},{1,3},{2,0},{3,1},{4,6},{5,7},{6,4},{7,5},{8,10},{9,11},{10,... | collective-permute-start | bytes 786440 | tf_op jit(solution)/shard_map/ppermute | solution.py:511
  25.5 11.6 %collective-permute-start.1 = (bf16[2,2,2,128,128]{4,3,2,1,0:T(8,128)(2,1)S(1)}, bf16[2,2,2,128,128]{4,3,2,1,0:T(8,128)(2,1)S(1)}, u32[]{:S(2)}, u32[]{:S(2)}) collective-permute-start(bf16[2,2,2,128,128]{4,3,2,1,0:T(8,128)(2,1)S(1)} %pad_maximum_fusion.rest_0_.rest_7_), channel_id=1, source_target_pairs={{0,4},{1,5},{2,6},{3,7},{4,0},{5,1},{6,2},{7,3},{8,12},{9,13},{10,... | collective-permute-start | bytes 786440 | tf_op jit(solution)/shard_map/ppermute | solution.py:511
  30.6 0.6 copy-start.2
  31.2 11.5 %copy-start.3 = (s32[2,4]{1,0:T(2,128)}, s32[2,4]{1,0:T(2,128)S(1)}, u32[]{:S(2)}) copy-start(s32[2,4]{1,0:T(2,128)S(1)} %get-tuple-element.58.counts) | copy-start | bytes 100
  31.2 20.6 %copy-start.1 = (bf16[2,2,8,128,128]{4,3,2,1,0:T(8,128)(2,1)S(1)}, bf16[2,2,8,128,128]{4,3,2,1,0:T(8,128)(2,1)}, u32[]{:S(2)}) copy-start(bf16[2,2,8,128,128]{4,3,2,1,0:T(8,128)(2,1)} %get-tuple-element.59.own) | copy-start | bytes 3145732
  37.1 14.6 %collective-permute-start.6 = (bf16[2,2,2,128,128]{4,3,2,1,0:T(8,128)(2,1)S(1)}, bf16[2,2,2,128,128]{4,3,2,1,0:T(8,128)(2,1)S(1)}, u32[]{:S(2)}, u32[]{:S(2)}) collective-permute-start(bf16[2,2,2,128,128]{4,3,2,1,0:T(8,128)(2,1)S(1)} %collective-permute-done.1.rest_1_.rest_0_.rest_9_), channel_id=1, source_target_pairs={{0,2},{1,3},{2,0},{3,1},{4,6},{5,7},{6,4},{7,5},{8,10},{9,11},{10,... | collective-permute-start | bytes 786440 | tf_op jit(solution)/shard_map/ppermute | solution.py:511
  39.6 8.1 %collective-permute-start.5 = (bf16[2,2,2,128,128]{4,3,2,1,0:T(8,128)(2,1)S(1)}, bf16[2,2,2,128,128]{4,3,2,1,0:T(8,128)(2,1)S(1)}, u32[]{:S(2)}, u32[]{:S(2)}) collective-permute-start(bf16[2,2,2,128,128]{4,3,2,1,0:T(8,128)(2,1)S(1)} %collective-permute-done.1.rest_1_.rest_0_.rest_9_), channel_id=1, source_target_pairs={{0,8},{8,16},{16,24},{1,9},{9,17},{17,25},{2,10},{10,18},{18,26},{... | collective-permute-start | bytes 786440 | tf_op jit(solution)/shard_map/ppermute | solution.py:517
  47.6 7.3 %collective-permute-start.7 = (bf16[2,2,2,128,128]{4,3,2,1,0:T(8,128)(2,1)S(1)}, bf16[2,2,2,128,128]{4,3,2,1,0:T(8,128)(2,1)S(1)}, u32[]{:S(2)}, u32[]{:S(2)}) collective-permute-start(bf16[2,2,2,128,128]{4,3,2,1,0:T(8,128)(2,1)S(1)} %collective-permute-done.2.rest_1_.rest_8_), channel_id=1, source_target_pairs={{0,8},{8,16},{16,24},{1,9},{9,17},{17,25},{2,10},{10,18},{18,26},{... | collective-permute-start | bytes 786440 | tf_op jit(solution)/shard_map/ppermute | solution.py:517
  51.7 5.6 %collective-permute-start.8 = (bf16[2,2,2,128,128]{4,3,2,1,0:T(8,128)(2,1)S(1)}, bf16[2,2,2,128,128]{4,3,2,1,0:T(8,128)(2,1)S(1)}, u32[]{:S(2)}, u32[]{:S(2)}) collective-permute-start(bf16[2,2,2,128,128]{4,3,2,1,0:T(8,128)(2,1)S(1)} %collective-permute-done.5.rest_2_.rest_5_), channel_id=1, source_target_pairs={{0,2},{1,3},{2,0},{3,1},{4,6},{5,7},{6,4},{7,5},{8,10},{9,11},{10,... | collective-permute-start | bytes 786440 | tf_op jit(solution)/shard_map/ppermute | solution.py:511
  75.8 5.3 %collective-permute-start.9 = (bf16[2,2,2,128,128]{4,3,2,1,0:T(8,128)(2,1)S(1)}, bf16[2,2,2,128,128]{4,3,2,1,0:T(8,128)(2,1)S(1)}, u32[]{:S(2)}, u32[]{:S(2)}) collective-permute-start(bf16[2,2,2,128,128]{4,3,2,1,0:T(8,128)(2,1)S(1)} %get-tuple-element.66), channel_id=1, source_target_pairs={{0,2},{1,3},{2,0},{3,1},{4,6},{5,7},{6,4},{7,5},{8,10},{9,11},{10,... | collective-permute-start | bytes 786440 | tf_op jit(solution)/shard_map/ppermute | solution.py:511
  75.9 18.3 %collective-permute-start.12 = (bf16[4,2,2,128,128]{4,3,2,1,0:T(8,128)(2,1)S(1)}, bf16[4,2,2,128,128]{4,3,2,1,0:T(8,128)(2,1)S(1)}, u32[]{:S(2)}, u32[]{:S(2)}) collective-permute-start(bf16[4,2,2,128,128]{4,3,2,1,0:T(8,128)(2,1)S(1)} %get-tuple-element.83), channel_id=1, source_target_pairs={{8,0},{16,8},{24,16},{9,1},{17,9},{25,17},{10,2},{18,10},{26,18},{... | collective-permute-start | bytes 1572872 | tf_op jit(solution)/shard_map/ppermute | solution.py:520
  81.2 14.3 %copy-start = (f32[320,128]{1,0:T(8,128)S(1)}, f32[320,128]{1,0:T(8,128)}, u32[]{:S(2)}) copy-start(f32[320,128]{1,0:T(8,128)} %constant.2.clone.refs_4_.rest_11_.rest_4_) | copy-start | bytes 491524
  81.2 12.8 %collective-permute-start.10 = (bf16[2,2,2,128,128]{4,3,2,1,0:T(8,128)(2,1)S(1)}, bf16[2,2,2,128,128]{4,3,2,1,0:T(8,128)(2,1)S(1)}, u32[]{:S(2)}, u32[]{:S(2)}) collective-permute-start(bf16[2,2,2,128,128]{4,3,2,1,0:T(8,128)(2,1)S(1)} %add_convert_fusion.2), channel_id=1, source_target_pairs={{8,0},{16,8},{24,16},{9,1},{17,9},{25,17},{10,2},{18,10},{26,18},{... | collective-permute-start | bytes 786440 | tf_op jit(solution)/shard_map/ppermute | solution.py:520
  83.3 10.8 %collective-permute-start.11 = (bf16[2,2,2,128,128]{4,3,2,1,0:T(8,128)(2,1)S(1)}, bf16[2,2,2,128,128]{4,3,2,1,0:T(8,128)(2,1)S(1)}, u32[]{:S(2)}, u32[]{:S(2)}) collective-permute-start(bf16[2,2,2,128,128]{4,3,2,1,0:T(8,128)(2,1)S(1)} %get-tuple-element.74), channel_id=1, source_target_pairs={{0,2},{1,3},{2,0},{3,1},{4,6},{5,7},{6,4},{7,5},{8,10},{9,11},{10,... | collective-permute-start | bytes 786440 | tf_op jit(solution)/shard_map/ppermute | solution.py:511
  94.2 17.6 %collective-permute-start.16 = (bf16[2,2,2,128,128]{4,3,2,1,0:T(8,128)(2,1)S(1)}, bf16[2,2,2,128,128]{4,3,2,1,0:T(8,128)(2,1)S(1)}, u32[]{:S(2)}, u32[]{:S(2)}) collective-permute-start(bf16[2,2,2,128,128]{4,3,2,1,0:T(8,128)(2,1)S(1)} %add_convert_fusion.1), channel_id=1, source_target_pairs={{0,4},{1,5},{2,6},{3,7},{4,0},{5,1},{6,2},{7,3},{8,12},{9,13},{10,... | collective-permute-start | bytes 786440 | tf_op jit(solution)/shard_map/ppermute | solution.py:511
  94.3 17.4 %collective-permute-start.15 = (bf16[2,2,2,128,128]{4,3,2,1,0:T(8,128)(2,1)S(1)}, bf16[2,2,2,128,128]{4,3,2,1,0:T(8,128)(2,1)S(1)}, u32[]{:S(2)}, u32[]{:S(2)}) collective-permute-start(bf16[2,2,2,128,128]{4,3,2,1,0:T(8,128)(2,1)S(1)} %add_convert_fusion), channel_id=1, source_target_pairs={{0,2},{1,3},{2,0},{3,1},{4,6},{5,7},{6,4},{7,5},{8,10},{9,11},{10,... | collective-permute-start | bytes 786440 | tf_op jit(solution)/shard_map/ppermute | solution.py:511
  106.4 7.7 %collective-permute-start.13 = (bf16[2,128,1024]{2,1,0:T(8,128)(2,1)S(1)}, bf16[2,128,1024]{2,1,0:T(8,128)(2,1)S(1)}, u32[]{:S(2)}, u32[]{:S(2)}) collective-permute-start(bf16[2,128,1024]{2,1,0:T(8,128)(2,1)S(1)} %get-tuple-element.89), channel_id=1, source_target_pairs={{0,1},{1,0},{2,3},{3,2},{4,5},{5,4},{6,7},{7,6},{8,9},{9,8},{10,11... | collective-permute-start | bytes 1572872 | tf_op jit(solution)/shard_map/ppermute | solution.py:511
  111.6 2.5 %collective-permute-start.14 = (bf16[2,128,1024]{2,1,0:T(8,128)(2,1)S(1)}, bf16[2,128,1024]{2,1,0:T(8,128)(2,1)S(1)}, u32[]{:S(2)}, u32[]{:S(2)}) collective-permute-start(bf16[2,128,1024]{2,1,0:T(8,128)(2,1)S(1)} %get-tuple-element.90), channel_id=1, source_target_pairs={{0,1},{1,0},{2,3},{3,2},{4,5},{5,4},{6,7},{7,6},{8,9},{9,8},{10,11... | collective-permute-start | bytes 1572872 | tf_op jit(solution)/shard_map/ppermute | solution.py:511
  112.6 1.5 %collective-permute-start.17 = (bf16[2,128,256]{2,1,0:T(8,128)(2,1)S(1)}, bf16[2,128,256]{2,1,0:T(8,128)(2,1)S(1)}, u32[]{:S(2)}, u32[]{:S(2)}) collective-permute-start(bf16[2,128,256]{2,1,0:T(8,128)(2,1)S(1)} %get-tuple-element.95), channel_id=1, source_target_pairs={{0,1},{1,0},{2,3},{3,2},{4,5},{5,4},{6,7},{7,6},{8,9},{9,8},{10,11... | collective-permute-start | bytes 393224 | tf_op jit(solution)/shard_map/ppermute | solution.py:511
